TPU v7x, 32 devices: a whole 2x2x4 slice. The times are simulated.
32 devices in a mesh: groups: 2 (over y), curve: 4 (over z), sub: 2 (over x), pair: 2 (over core).
Axes of the slice: x: 2, y: 2, z: 4, core: 2. Of those that a mesh axis runs over, the one named last changes fastest.
Arguments:
- old_dynamics: float32 [10, 128, 4096], P('groups', 'curve', ('sub', 'pair')), parts along dimension 0, may hold values from -6 to 6
- old_area: float32 [10, 128, 4096], P('groups', 'curve', ('sub', 'pair')), parts along dimension 0, may hold values from 0.02 to 0.19
- old_volume: float32 [10, 128, 4096], P('groups', 'curve', ('sub', 'pair')), parts along dimension 0, may hold values from 0.05 to 1
- old_block: int32 [128], replicated, may hold values from 0 to 127, as said below
- wind_stress: float32 [2, 1024, 1024], P(None, ('groups', 'curve'), ('sub', 'pair')), parts along dimension 1, may hold values from -6 to 6
- ice_mask: int32 [1024, 1024], P(('groups', 'curve'), ('sub', 'pair')), parts along dimension 0, may hold values 0 or 1
Outputs:
- velocity: float32 [2, 1024, 1024], P(None, ('groups', 'curve'), ('sub', 'pair')), parts along dimension 1
- stress: float32 [3, 1024, 1024], P(None, ('groups', 'curve'), ('sub', 'pair')), parts along dimension 1
There are 2 independent parts, one for each index of `groups`. A program takes and returns all parts, laid end to end along the dimension named above; an argument that names none is the same for every part. Nothing has to cross between parts.
Inputs may be any that keep to these rules, and one draw needn't show every extreme that they name: `old_block`: A permutation: entry i names the block in old slot i, which lies on curve owner i // 32; block b belongs to new owner b // 32 and has the same slot number b % (32) in both layouts. Each owner sends exactly 2 blocks to each of 3 other owners and keeps the rest.
All inputs are finite; a program needn't handle non-finite values. No bound on the sum of `ice_mask` on one device may be relied on, other than what follows from the above.
Results may differ from a plain program's by a relative error of at most 0.00002.
Values sent between devices are 32-bit elements; how exact they have to be, the bound alone decides.
A program may use at most 64 MiB of HBM per device.

v0:
```python
import jax
import jax.numpy as jnp
from jax import lax
from jax.sharding import PartitionSpec as P

BS = 32
RB = 4
CB = 8
SUB = 6
MOST = 2


def padded_2(value, sides, width):
    for axis, dim in sides:
        size, length = (lax.axis_size(axis), value.shape[dim])
        up = [(i, (i + 1) % size) for i in range(size - 1)]
        down = [(j, i) for i, j in up]
        last = lax.slice_in_dim(value, length - width, length, axis=dim)
        initial = lax.slice_in_dim(value, 0, width, axis=dim)
        before = lax.ppermute(last, axis, up)
        after = lax.ppermute(initial, axis, down)
        value = jnp.concatenate([before, value, after], axis=dim)
    return value


def derive(area, volume):
    total_area = jnp.sum(area, axis=0)
    total_volume = jnp.sum(volume, axis=0)
    strength = 2.0 * total_volume * jnp.exp(-2.0 * (1.0 - total_area))
    return jnp.stack([strength, total_volume])


def new_stress(velocity_pad, stress, strength, active):
    along_x = velocity_pad[0]
    along_y = velocity_pad[1]
    du_dx = 0.5 * (along_x[1:-1, 2:] - along_x[1:-1, :-2])
    du_dy = 0.5 * (along_x[2:, 1:-1] - along_x[:-2, 1:-1])
    dv_dx = 0.5 * (along_y[1:-1, 2:] - along_y[1:-1, :-2])
    dv_dy = 0.5 * (along_y[2:, 1:-1] - along_y[:-2, 1:-1])
    divergence = du_dx + dv_dy
    tension = du_dx - dv_dy
    shearing = du_dy + dv_dx
    deformation = jnp.sqrt(
        divergence * divergence + 0.25 * (tension * tension + shearing * shearing) + 0.25
    )
    pressure = strength / deformation
    first = active * (stress[0] + 0.5 * pressure * (divergence - deformation)) / 1.5
    second = active * (stress[1] + 0.125 * pressure * tension) / 1.5
    third = active * (stress[2] + 0.0625 * pressure * shearing) / 1.5
    return jnp.stack([first, second, third])


def new_velocity(stress_pad, velocity, ice_mass, wind_stress, active):
    stress_xx = 0.5 * (stress_pad[0] + stress_pad[1])
    stress_yy = 0.5 * (stress_pad[0] - stress_pad[1])
    stress_xy = stress_pad[2]
    force_x = 0.5 * (stress_xx[1:-1, 2:] - stress_xx[1:-1, :-2]) + 0.5 * (
        stress_xy[2:, 1:-1] - stress_xy[:-2, 1:-1]
    )
    force_y = 0.5 * (stress_xy[1:-1, 2:] - stress_xy[1:-1, :-2]) + 0.5 * (
        stress_yy[2:, 1:-1] - stress_yy[:-2, 1:-1]
    )
    drag = ice_mass + 0.5
    turning = 0.5 * ice_mass
    determinant = drag * drag + turning * turning
    rhs_x = ice_mass * velocity[0] + force_x + wind_stress[0]
    rhs_y = ice_mass * velocity[1] + force_y + wind_stress[1]
    return jnp.stack(
        [
            active * (drag * rhs_x + turning * rhs_y) / determinant,
            active * (drag * rhs_y - turning * rhs_x) / determinant,
        ]
    )


def to_grid(blocks):
    field_count = blocks.shape[0]
    shaped = blocks.reshape(field_count, RB, CB, BS, BS)
    return shaped.transpose(0, 1, 3, 2, 4).reshape(field_count, RB * BS, CB * BS)


def shards(old_dynamics, old_area, old_volume, old_block, wind_stress, ice_mask):
    owners = lax.axis_size("curve")
    myself = lax.axis_index("curve")
    slot_count = RB * CB
    owner_table = (old_block // slot_count).reshape(owners, slot_count)
    sources = jnp.arange(owners, dtype=jnp.int32)
    slot_ids = jnp.arange(slot_count, dtype=jnp.int32)
    rank_ids = jnp.arange(MOST, dtype=jnp.int32)
    elsewhere = (sources != myself)[:, None]
    target = lax.dynamic_index_in_dim(owner_table, myself, 0, keepdims=False)
    send_match = (target[None, :] == sources[:, None]) & elsewhere
    send_rank = jnp.cumsum(send_match.astype(jnp.int32), axis=1) - 1
    chosen = send_match[:, None, :] & (send_rank[:, None, :] == rank_ids[None, :, None])
    send_index = jnp.sum(jnp.where(chosen, slot_ids[None, None, :], 0), axis=2)
    send_index = send_index + slot_count * (1 - jnp.any(chosen, axis=2).astype(jnp.int32))
    send_index = send_index.reshape(-1)
    recv_match = (owner_table == myself) & elsewhere
    recv_rank = jnp.cumsum(recv_match.astype(jnp.int32), axis=1) - 1
    source_pos = jnp.sum(jnp.where(recv_match, sources[:, None] * MOST + recv_rank, 0), axis=0)
    arrived = jnp.any(recv_match, axis=0)

    def pack_out(blocks):
        padded = jnp.concatenate([blocks, jnp.zeros_like(blocks[:, :1])], axis=1)
        return jnp.take(padded, send_index, axis=1)

    def place_in(came, blocks):
        return jnp.where(arrived[None, :, None], jnp.take(came, source_pos, axis=1), blocks)

    came_dynamics, came_area, came_volume = (
        lax.all_to_all(pack_out(old_dynamics), "curve", split_axis=1, concat_axis=1, tiled=True),
        lax.all_to_all(pack_out(old_area), "curve", split_axis=1, concat_axis=1, tiled=True),
        lax.all_to_all(pack_out(old_volume), "curve", split_axis=1, concat_axis=1, tiled=True),
    )
    dynamics = place_in(came_dynamics, old_dynamics)
    derived = derive(place_in(came_area, old_area), place_in(came_volume, old_volume))
    dynamics = to_grid(dynamics)
    derived = to_grid(derived)
    strength = derived[0]
    ice_mass = derived[1]
    active = ice_mask.astype(jnp.float32)
    velocity = dynamics[0:2]
    stress = dynamics[2:5]
    for subcycle in range(SUB):
        velocity_pad = padded_2(velocity, (("curve", 1), (("sub", "pair"), 2)), 1)
        stress = new_stress(velocity_pad, stress, strength, active)
        stress_pad = padded_2(stress, (("curve", 1), (("sub", "pair"), 2)), 1)
        velocity = new_velocity(stress_pad, velocity, ice_mass, wind_stress, active)
    return (velocity, stress)


def solution(mesh):
    return jax.shard_map(
        shards,
        mesh=mesh,
        in_specs=(
            P("groups", "curve", ("sub", "pair")),
            P("groups", "curve", ("sub", "pair")),
            P("groups", "curve", ("sub", "pair")),
            P(),
            P(None, ("groups", "curve"), ("sub", "pair")),
            P(("groups", "curve"), ("sub", "pair")),
        ),
        out_specs=(
            P(None, ("groups", "curve"), ("sub", "pair")),
            P(None, ("groups", "curve"), ("sub", "pair")),
        ),
        check_vma=False,
    )
```

profile of v0, /device:TPU:1, one launch (start us, length us, event | category | flops | bytes accessed | tf_op | source)
XLA Modules:
  0.0 265.6 jit_solution(7101780734389336536)
XLA Ops:
  7.7 5.4 %all-to-all-start.1 = ((f32[5,8,1024]{2,0,1:T(8,128)}), f32[5,8,1024]{2,0,1:T(8,128)S(1)}, u32[]{:S(2)}, u32[]{:S(2)}) async-start(f32[5,8,1024]{2,0,1:T(8,128)} %get-tuple-element.145), calls=%async_computation.1 | async-start | bytes 524288 | tf_op jit(solution)/shard_map/all_to_all | solution.py:112
  13.3 7.3 %all-to-all-done.1 = f32[5,8,1024]{2,0,1:T(8,128)S(1)} async-done(((f32[5,8,1024]{2,0,1:T(8,128)}), f32[5,8,1024]{2,0,1:T(8,128)S(1)}, u32[]{:S(2)}, u32[]{:S(2)}) %all-to-all-start.1) | async-done | bytes 163872 | tf_op jit(solution)/shard_map/all_to_all | solution.py:112
  20.6 3.4 %all-to-all-start = ((f32[5,8,1024]{2,0,1:T(8,128)}), f32[5,8,1024]{2,0,1:T(8,128)S(1)}, u32[]{:S(2)}, u32[]{:S(2)}) async-start(f32[5,8,1024]{2,0,1:T(8,128)} %get-tuple-element.146), calls=%async_computation | async-start | bytes 524288 | tf_op jit(solution)/shard_map/all_to_all | solution.py:113
  24.1 5.5 %all-to-all-done = f32[5,8,1024]{2,0,1:T(8,128)S(1)} async-done(((f32[5,8,1024]{2,0,1:T(8,128)}), f32[5,8,1024]{2,0,1:T(8,128)S(1)}, u32[]{:S(2)}, u32[]{:S(2)}) %all-to-all-start) | async-done | bytes 163872 | tf_op jit(solution)/shard_map/all_to_all | solution.py:113
  29.7 3.4 %all-to-all-start.2 = ((f32[5,8,1024]{2,0,1:T(8,128)}), f32[5,8,1024]{2,0,1:T(8,128)S(1)}, u32[]{:S(2)}, u32[]{:S(2)}) async-start(f32[5,8,1024]{2,0,1:T(8,128)} %get-tuple-element.144), calls=%async_computation.2 | async-start | bytes 524288 | tf_op jit(solution)/shard_map/all_to_all | solution.py:111
  34.4 4.3 %all-to-all-done.2 = f32[5,8,1024]{2,0,1:T(8,128)S(1)} async-done(((f32[5,8,1024]{2,0,1:T(8,128)}), f32[5,8,1024]{2,0,1:T(8,128)S(1)}, u32[]{:S(2)}, u32[]{:S(2)}) %all-to-all-start.2) | async-done | bytes 163872 | tf_op jit(solution)/shard_map/all_to_all | solution.py:111
  40.3 3.9 %fusion = (f32[32,1024]{1,0:T(8,128)S(1)}, f32[32,1024]{1,0:T(8,128)S(1)}, f32[5,32,1024]{2,0,1:T(8,128)S(1)}) fusion(f32[32,5,1024]{2,1,0:T(8,128)S(1)} %gather_fusion.3, pred[32]{0:T(512)(128)(4,1)S(1)} %compare_and_fusion, pred[32]{0:T(512)(128)(4,1)S(1)} %get-tuple-element.42, f32[5,32,1024]{2,1,0:T(8,128)} %param.11, f32[5,32,1024]{2,1,0:T(8,128)} %param.12, ...), kind=kLoop, calls=%fused_computation.9 | loop fusion | flops 1245184 | bytes 4849728 | tf_op jit(solution)/shard_map/reduce_sum | solution.py:27
  57.7 9.3 %collective-permute-start.2 = (f32[2,130,1]{2,1,0:T(8,128)S(1)}, f32[2,130,1]{2,1,0:T(8,128)S(1)}, u32[]{:S(2)}, u32[]{:S(2)}) collective-permute-start(f32[2,130,1]{2,1,0:T(8,128)S(1)} %get-tuple-element.117), channel_id=1, source_target_pairs={{0,1},{1,2},{2,3},{4,5},{5,6},{6,7},{8,9},{9,10},{10,11},{12,13},{... | collective-permute-start | bytes 3128 | tf_op jit(solution)/shard_map/ppermute | solution.py:20
  82.1 3.5 %collective-permute-start.6 = (f32[3,130,1]{2,1,0:T(8,128)}, f32[3,130,1]{2,1,0:T(8,128)}, u32[]{:S(2)}, u32[]{:S(2)}) collective-permute-start(f32[3,130,1]{2,1,0:T(8,128)} %get-tuple-element.91), channel_id=1, source_target_pairs={{0,1},{1,2},{2,3},{4,5},{5,6},{6,7},{8,9},{9,10},{10,11},{12,13},{... | collective-permute-start | bytes 4688 | tf_op jit(solution)/shard_map/ppermute | solution.py:20
  89.6 3.2 %collective-permute-done.7 = f32[3,130,1]{2,1,0:T(8,128)} collective-permute-done((f32[3,130,1]{2,1,0:T(8,128)S(1)}, f32[3,130,1]{2,1,0:T(8,128)}, u32[]{:S(2)}, u32[]{:S(2)}) %collective-permute-start.7) | collective-permute-done | bytes 1592 | tf_op jit(solution)/shard_map/ppermute | solution.py:21
  94.6 3.4 %collective-permute-start.8 = (f32[2,1,256]{2,1,0:T(1,128)S(1)}, f32[2,1,256]{2,1,0:T(1,128)S(1)}, u32[]{:S(2)}, u32[]{:S(2)}) collective-permute-start(f32[2,1,256]{2,1,0:T(1,128)S(1)} %get-tuple-element.137), channel_id=1, source_target_pairs={{0,4},{4,8},{8,12},{1,5},{5,9},{9,13},{2,6},{6,10},{10,14},{3,7},{... | collective-permute-start | bytes 6152 | tf_op jit(solution)/shard_map/ppermute | solution.py:20
  107.6 4.4 %collective-permute-done.11 = f32[2,130,1]{2,1,0:T(8,128)S(1)} collective-permute-done((f32[2,130,1]{2,1,0:T(8,128)S(1)}, f32[2,130,1]{2,1,0:T(8,128)S(1)}, u32[]{:S(2)}, u32[]{:S(2)}) %collective-permute-start.11) | collective-permute-done | bytes 1072 | tf_op jit(solution)/shard_map/ppermute | solution.py:21
  118.9 3.2 %collective-permute-start.14 = (f32[3,130,1]{2,1,0:T(8,128)S(1)}, f32[3,130,1]{2,1,0:T(8,128)S(1)}, u32[]{:S(2)}, u32[]{:S(2)}) collective-permute-start(f32[3,130,1]{2,1,0:T(8,128)S(1)} %get-tuple-element.87), channel_id=1, source_target_pairs={{0,1},{1,2},{2,3},{4,5},{5,6},{6,7},{8,9},{9,10},{10,11},{12,13},{... | collective-permute-start | bytes 4688 | tf_op jit(solution)/shard_map/ppermute | solution.py:20
  124.9 4.4 %collective-permute-done.15 = f32[3,130,1]{2,1,0:T(8,128)S(1)} collective-permute-done((f32[3,130,1]{2,1,0:T(8,128)S(1)}, f32[3,130,1]{2,1,0:T(8,128)S(1)}, u32[]{:S(2)}, u32[]{:S(2)}) %collective-permute-start.15) | collective-permute-done | bytes 1592 | tf_op jit(solution)/shard_map/ppermute | solution.py:21
  141.3 4.4 %collective-permute-done.19 = f32[2,130,1]{2,1,0:T(8,128)S(1)} collective-permute-done((f32[2,130,1]{2,1,0:T(8,128)S(1)}, f32[2,130,1]{2,1,0:T(8,128)S(1)}, u32[]{:S(2)}, u32[]{:S(2)}) %collective-permute-start.19) | collective-permute-done | bytes 1072 | tf_op jit(solution)/shard_map/ppermute | solution.py:21
  158.6 4.4 %collective-permute-done.23 = f32[3,130,1]{2,1,0:T(8,128)S(1)} collective-permute-done((f32[3,130,1]{2,1,0:T(8,128)S(1)}, f32[3,130,1]{2,1,0:T(8,128)S(1)}, u32[]{:S(2)}, u32[]{:S(2)}) %collective-permute-start.23) | collective-permute-done | bytes 1592 | tf_op jit(solution)/shard_map/ppermute | solution.py:21
  175.0 4.4 %collective-permute-done.27 = f32[2,130,1]{2,1,0:T(8,128)S(1)} collective-permute-done((f32[2,130,1]{2,1,0:T(8,128)S(1)}, f32[2,130,1]{2,1,0:T(8,128)S(1)}, u32[]{:S(2)}, u32[]{:S(2)}) %collective-permute-start.27) | collective-permute-done | bytes 1072 | tf_op jit(solution)/shard_map/ppermute | solution.py:21
  192.3 4.4 %collective-permute-done.31 = f32[3,130,1]{2,1,0:T(8,128)S(1)} collective-permute-done((f32[3,130,1]{2,1,0:T(8,128)S(1)}, f32[3,130,1]{2,1,0:T(8,128)S(1)}, u32[]{:S(2)}, u32[]{:S(2)}) %collective-permute-start.31) | collective-permute-done | bytes 1592 | tf_op jit(solution)/shard_map/ppermute | solution.py:21
  208.7 4.4 %collective-permute-done.35 = f32[2,130,1]{2,1,0:T(8,128)S(1)} collective-permute-done((f32[2,130,1]{2,1,0:T(8,128)S(1)}, f32[2,130,1]{2,1,0:T(8,128)S(1)}, u32[]{:S(2)}, u32[]{:S(2)}) %collective-permute-start.35) | collective-permute-done | bytes 1072 | tf_op jit(solution)/shard_map/ppermute | solution.py:21
  220.0 3.2 %collective-permute-start.38 = (f32[3,130,1]{2,1,0:T(8,128)S(1)}, f32[3,130,1]{2,1,0:T(8,128)S(1)}, u32[]{:S(2)}, u32[]{:S(2)}) collective-permute-start(f32[3,130,1]{2,1,0:T(8,128)S(1)} %get-tuple-element.75), channel_id=1, source_target_pairs={{0,1},{1,2},{2,3},{4,5},{5,6},{6,7},{8,9},{9,10},{10,11},{12,13},{... | collective-permute-start | bytes 4688 | tf_op jit(solution)/shard_map/ppermute | solution.py:20
  226.0 4.4 %collective-permute-done.39 = f32[3,130,1]{2,1,0:T(8,128)S(1)} collective-permute-done((f32[3,130,1]{2,1,0:T(8,128)S(1)}, f32[3,130,1]{2,1,0:T(8,128)S(1)}, u32[]{:S(2)}, u32[]{:S(2)}) %collective-permute-start.39) | collective-permute-done | bytes 1592 | tf_op jit(solution)/shard_map/ppermute | solution.py:21
  242.4 4.4 %collective-permute-done.43 = f32[2,130,1]{2,1,0:T(8,128)S(1)} collective-permute-done((f32[2,130,1]{2,1,0:T(8,128)S(1)}, f32[2,130,1]{2,1,0:T(8,128)S(1)}, u32[]{:S(2)}, u32[]{:S(2)}) %collective-permute-start.43) | collective-permute-done | bytes 1072 | tf_op jit(solution)/shard_map/ppermute | solution.py:21
  253.8 3.2 %collective-permute-start.46 = (f32[3,130,1]{2,1,0:T(8,128)S(1)}, f32[3,130,1]{2,1,0:T(8,128)S(1)}, u32[]{:S(2)}, u32[]{:S(2)}) collective-permute-start(f32[3,130,1]{2,1,0:T(8,128)S(1)} %get-tuple-element.71), channel_id=1, source_target_pairs={{0,1},{1,2},{2,3},{4,5},{5,6},{6,7},{8,9},{9,10},{10,11},{12,13},{... | collective-permute-start | bytes 4688 | tf_op jit(solution)/shard_map/ppermute | solution.py:20
  259.7 4.4 %collective-permute-done.47 = f32[3,130,1]{2,1,0:T(8,128)S(1)} collective-permute-done((f32[3,130,1]{2,1,0:T(8,128)S(1)}, f32[3,130,1]{2,1,0:T(8,128)S(1)}, u32[]{:S(2)}, u32[]{:S(2)}) %collective-permute-start.47) | collective-permute-done | bytes 1592 | tf_op jit(solution)/shard_map/ppermute | solution.py:21
  (250 shorter events, 157.4 us)
Async XLA Ops:
  7.7 13.0 %all-to-all-start.1 = ((f32[5,8,1024]{2,0,1:T(8,128)}), f32[5,8,1024]{2,0,1:T(8,128)S(1)}, u32[]{:S(2)}, u32[]{:S(2)}) async-start(f32[5,8,1024]{2,0,1:T(8,128)} %get-tuple-element.145), calls=%async_computation.1 | async-start | bytes 524288 | tf_op jit(solution)/shard_map/all_to_all | solution.py:112
  20.6 9.0 %all-to-all-start = ((f32[5,8,1024]{2,0,1:T(8,128)}), f32[5,8,1024]{2,0,1:T(8,128)S(1)}, u32[]{:S(2)}, u32[]{:S(2)}) async-start(f32[5,8,1024]{2,0,1:T(8,128)} %get-tuple-element.146), calls=%async_computation | async-start | bytes 524288 | tf_op jit(solution)/shard_map/all_to_all | solution.py:113
  29.7 9.0 %all-to-all-start.2 = ((f32[5,8,1024]{2,0,1:T(8,128)}), f32[5,8,1024]{2,0,1:T(8,128)S(1)}, u32[]{:S(2)}, u32[]{:S(2)}) async-start(f32[5,8,1024]{2,0,1:T(8,128)} %get-tuple-element.144), calls=%async_computation.2 | async-start | bytes 524288 | tf_op jit(solution)/shard_map/all_to_all | solution.py:111
  57.7 14.2 %collective-permute-start.2 = (f32[2,130,1]{2,1,0:T(8,128)S(1)}, f32[2,130,1]{2,1,0:T(8,128)S(1)}, u32[]{:S(2)}, u32[]{:S(2)}) collective-permute-start(f32[2,130,1]{2,1,0:T(8,128)S(1)} %get-tuple-element.117), channel_id=1, source_target_pairs={{0,1},{1,2},{2,3},{4,5},{5,6},{6,7},{8,9},{9,10},{10,11},{12,13},{... | collective-permute-start | bytes 3128 | tf_op jit(solution)/shard_map/ppermute | solution.py:20
  67.0 6.5 %collective-permute-start.3 = (f32[2,130,1]{2,1,0:T(8,128)S(1)}, f32[2,130,1]{2,1,0:T(8,128)}, u32[]{:S(2)}, u32[]{:S(2)}) collective-permute-start(f32[2,130,1]{2,1,0:T(8,128)S(1)} %get-tuple-element.118), channel_id=1, source_target_pairs={{1,0},{2,1},{3,2},{5,4},{6,5},{7,6},{9,8},{10,9},{11,10},{13,12},{... | collective-permute-start | bytes 3128 | tf_op jit(solution)/shard_map/ppermute | solution.py:21
  82.1 7.5 %collective-permute-start.6 = (f32[3,130,1]{2,1,0:T(8,128)}, f32[3,130,1]{2,1,0:T(8,128)}, u32[]{:S(2)}, u32[]{:S(2)}) collective-permute-start(f32[3,130,1]{2,1,0:T(8,128)} %get-tuple-element.91), channel_id=1, source_target_pairs={{0,1},{1,2},{2,3},{4,5},{5,6},{6,7},{8,9},{9,10},{10,11},{12,13},{... | collective-permute-start | bytes 4688 | tf_op jit(solution)/shard_map/ppermute | solution.py:20
  85.6 7.2 %collective-permute-start.7 = (f32[3,130,1]{2,1,0:T(8,128)S(1)}, f32[3,130,1]{2,1,0:T(8,128)}, u32[]{:S(2)}, u32[]{:S(2)}) collective-permute-start(f32[3,130,1]{2,1,0:T(8,128)S(1)} %get-tuple-element.92), channel_id=1, source_target_pairs={{1,0},{2,1},{3,2},{5,4},{6,5},{7,6},{9,8},{10,9},{11,10},{13,12},{... | collective-permute-start | bytes 4688 | tf_op jit(solution)/shard_map/ppermute | solution.py:21
  105.6 6.4 %collective-permute-start.11 = (f32[2,130,1]{2,1,0:T(8,128)S(1)}, f32[2,130,1]{2,1,0:T(8,128)S(1)}, u32[]{:S(2)}, u32[]{:S(2)}) collective-permute-start(f32[2,130,1]{2,1,0:T(8,128)S(1)} %get-tuple-element.116), channel_id=1, source_target_pairs={{1,0},{2,1},{3,2},{5,4},{6,5},{7,6},{9,8},{10,9},{11,10},{13,12},{... | collective-permute-start | bytes 3128 | tf_op jit(solution)/shard_map/ppermute | solution.py:21
  118.9 5.9 %collective-permute-start.14 = (f32[3,130,1]{2,1,0:T(8,128)S(1)}, f32[3,130,1]{2,1,0:T(8,128)S(1)}, u32[]{:S(2)}, u32[]{:S(2)}) collective-permute-start(f32[3,130,1]{2,1,0:T(8,128)S(1)} %get-tuple-element.87), channel_id=1, source_target_pairs={{0,1},{1,2},{2,3},{4,5},{5,6},{6,7},{8,9},{9,10},{10,11},{12,13},{... | collective-permute-start | bytes 4688 | tf_op jit(solution)/shard_map/ppermute | solution.py:20
  122.1 7.1 %collective-permute-start.15 = (f32[3,130,1]{2,1,0:T(8,128)S(1)}, f32[3,130,1]{2,1,0:T(8,128)S(1)}, u32[]{:S(2)}, u32[]{:S(2)}) collective-permute-start(f32[3,130,1]{2,1,0:T(8,128)S(1)} %get-tuple-element.88), channel_id=1, source_target_pairs={{1,0},{2,1},{3,2},{5,4},{6,5},{7,6},{9,8},{10,9},{11,10},{13,12},{... | collective-permute-start | bytes 4688 | tf_op jit(solution)/shard_map/ppermute | solution.py:21
  136.1 5.2 %collective-permute-start.18 = (f32[2,130,1]{2,1,0:T(8,128)S(1)}, f32[2,130,1]{2,1,0:T(8,128)S(1)}, u32[]{:S(2)}, u32[]{:S(2)}) collective-permute-start(f32[2,130,1]{2,1,0:T(8,128)S(1)} %get-tuple-element.113), channel_id=1, source_target_pairs={{0,1},{1,2},{2,3},{4,5},{5,6},{6,7},{8,9},{9,10},{10,11},{12,13},{... | collective-permute-start | bytes 3128 | tf_op jit(solution)/shard_map/ppermute | solution.py:20
  139.3 6.4 %collective-permute-start.19 = (f32[2,130,1]{2,1,0:T(8,128)S(1)}, f32[2,130,1]{2,1,0:T(8,128)S(1)}, u32[]{:S(2)}, u32[]{:S(2)}) collective-permute-start(f32[2,130,1]{2,1,0:T(8,128)S(1)} %get-tuple-element.114), channel_id=1, source_target_pairs={{1,0},{2,1},{3,2},{5,4},{6,5},{7,6},{9,8},{10,9},{11,10},{13,12},{... | collective-permute-start | bytes 3128 | tf_op jit(solution)/shard_map/ppermute | solution.py:21
  152.6 5.9 %collective-permute-start.22 = (f32[3,130,1]{2,1,0:T(8,128)S(1)}, f32[3,130,1]{2,1,0:T(8,128)S(1)}, u32[]{:S(2)}, u32[]{:S(2)}) collective-permute-start(f32[3,130,1]{2,1,0:T(8,128)S(1)} %get-tuple-element.83), channel_id=1, source_target_pairs={{0,1},{1,2},{2,3},{4,5},{5,6},{6,7},{8,9},{9,10},{10,11},{12,13},{... | collective-permute-start | bytes 4688 | tf_op jit(solution)/shard_map/ppermute | solution.py:20
  155.8 7.1 %collective-permute-start.23 = (f32[3,130,1]{2,1,0:T(8,128)S(1)}, f32[3,130,1]{2,1,0:T(8,128)S(1)}, u32[]{:S(2)}, u32[]{:S(2)}) collective-permute-start(f32[3,130,1]{2,1,0:T(8,128)S(1)} %get-tuple-element.84), channel_id=1, source_target_pairs={{1,0},{2,1},{3,2},{5,4},{6,5},{7,6},{9,8},{10,9},{11,10},{13,12},{... | collective-permute-start | bytes 4688 | tf_op jit(solution)/shard_map/ppermute | solution.py:21
  173.0 6.4 %collective-permute-start.27 = (f32[2,130,1]{2,1,0:T(8,128)S(1)}, f32[2,130,1]{2,1,0:T(8,128)S(1)}, u32[]{:S(2)}, u32[]{:S(2)}) collective-permute-start(f32[2,130,1]{2,1,0:T(8,128)S(1)} %get-tuple-element.112), channel_id=1, source_target_pairs={{1,0},{2,1},{3,2},{5,4},{6,5},{7,6},{9,8},{10,9},{11,10},{13,12},{... | collective-permute-start | bytes 3128 | tf_op jit(solution)/shard_map/ppermute | solution.py:21
  186.3 5.9 %collective-permute-start.30 = (f32[3,130,1]{2,1,0:T(8,128)S(1)}, f32[3,130,1]{2,1,0:T(8,128)S(1)}, u32[]{:S(2)}, u32[]{:S(2)}) collective-permute-start(f32[3,130,1]{2,1,0:T(8,128)S(1)} %get-tuple-element.79), channel_id=1, source_target_pairs={{0,1},{1,2},{2,3},{4,5},{5,6},{6,7},{8,9},{9,10},{10,11},{12,13},{... | collective-permute-start | bytes 4688 | tf_op jit(solution)/shard_map/ppermute | solution.py:20
  189.5 7.1 %collective-permute-start.31 = (f32[3,130,1]{2,1,0:T(8,128)S(1)}, f32[3,130,1]{2,1,0:T(8,128)S(1)}, u32[]{:S(2)}, u32[]{:S(2)}) collective-permute-start(f32[3,130,1]{2,1,0:T(8,128)S(1)} %get-tuple-element.80), channel_id=1, source_target_pairs={{1,0},{2,1},{3,2},{5,4},{6,5},{7,6},{9,8},{10,9},{11,10},{13,12},{... | collective-permute-start | bytes 4688 | tf_op jit(solution)/shard_map/ppermute | solution.py:21
  206.7 6.4 %collective-permute-start.35 = (f32[2,130,1]{2,1,0:T(8,128)S(1)}, f32[2,130,1]{2,1,0:T(8,128)S(1)}, u32[]{:S(2)}, u32[]{:S(2)}) collective-permute-start(f32[2,130,1]{2,1,0:T(8,128)S(1)} %get-tuple-element.110), channel_id=1, source_target_pairs={{1,0},{2,1},{3,2},{5,4},{6,5},{7,6},{9,8},{10,9},{11,10},{13,12},{... | collective-permute-start | bytes 3128 | tf_op jit(solution)/shard_map/ppermute | solution.py:21
  220.0 5.9 %collective-permute-start.38 = (f32[3,130,1]{2,1,0:T(8,128)S(1)}, f32[3,130,1]{2,1,0:T(8,128)S(1)}, u32[]{:S(2)}, u32[]{:S(2)}) collective-permute-start(f32[3,130,1]{2,1,0:T(8,128)S(1)} %get-tuple-element.75), channel_id=1, source_target_pairs={{0,1},{1,2},{2,3},{4,5},{5,6},{6,7},{8,9},{9,10},{10,11},{12,13},{... | collective-permute-start | bytes 4688 | tf_op jit(solution)/shard_map/ppermute | solution.py:20
  223.2 7.1 %collective-permute-start.39 = (f32[3,130,1]{2,1,0:T(8,128)S(1)}, f32[3,130,1]{2,1,0:T(8,128)S(1)}, u32[]{:S(2)}, u32[]{:S(2)}) collective-permute-start(f32[3,130,1]{2,1,0:T(8,128)S(1)} %get-tuple-element.76), channel_id=1, source_target_pairs={{1,0},{2,1},{3,2},{5,4},{6,5},{7,6},{9,8},{10,9},{11,10},{13,12},{... | collective-permute-start | bytes 4688 | tf_op jit(solution)/shard_map/ppermute | solution.py:21
  237.2 5.2 %collective-permute-start.42 = (f32[2,130,1]{2,1,0:T(8,128)S(1)}, f32[2,130,1]{2,1,0:T(8,128)S(1)}, u32[]{:S(2)}, u32[]{:S(2)}) collective-permute-start(f32[2,130,1]{2,1,0:T(8,128)S(1)} %get-tuple-element.107), channel_id=1, source_target_pairs={{0,1},{1,2},{2,3},{4,5},{5,6},{6,7},{8,9},{9,10},{10,11},{12,13},{... | collective-permute-start | bytes 3128 | tf_op jit(solution)/shard_map/ppermute | solution.py:20
  240.4 6.4 %collective-permute-start.43 = (f32[2,130,1]{2,1,0:T(8,128)S(1)}, f32[2,130,1]{2,1,0:T(8,128)S(1)}, u32[]{:S(2)}, u32[]{:S(2)}) collective-permute-start(f32[2,130,1]{2,1,0:T(8,128)S(1)} %get-tuple-element.108), channel_id=1, source_target_pairs={{1,0},{2,1},{3,2},{5,4},{6,5},{7,6},{9,8},{10,9},{11,10},{13,12},{... | collective-permute-start | bytes 3128 | tf_op jit(solution)/shard_map/ppermute | solution.py:21
  253.8 5.9 %collective-permute-start.46 = (f32[3,130,1]{2,1,0:T(8,128)S(1)}, f32[3,130,1]{2,1,0:T(8,128)S(1)}, u32[]{:S(2)}, u32[]{:S(2)}) collective-permute-start(f32[3,130,1]{2,1,0:T(8,128)S(1)} %get-tuple-element.71), channel_id=1, source_target_pairs={{0,1},{1,2},{2,3},{4,5},{5,6},{6,7},{8,9},{9,10},{10,11},{12,13},{... | collective-permute-start | bytes 4688 | tf_op jit(solution)/shard_map/ppermute | solution.py:20
  257.0 7.1 %collective-permute-start.47 = (f32[3,130,1]{2,1,0:T(8,128)S(1)}, f32[3,130,1]{2,1,0:T(8,128)S(1)}, u32[]{:S(2)}, u32[]{:S(2)}) collective-permute-start(f32[3,130,1]{2,1,0:T(8,128)S(1)} %get-tuple-element.72), channel_id=1, source_target_pairs={{1,0},{2,1},{3,2},{5,4},{6,5},{7,6},{9,8},{10,9},{11,10},{13,12},{... | collective-permute-start | bytes 4688 | tf_op jit(solution)/shard_map/ppermute | solution.py:21
  (39 other events, 153.7 us)
where the time goes:
time: 267 us; the launch traced here: 266 us
  starting transfers between devices  118 us (44%)
  waiting for transfers between devices  106 us (40%)
  local copies, waits for them, and re-layouts  20.2 us (8%)
  other arithmetic  18.6 us (7%)
    ppermute x24, waiting for transfers between devices, padded_2(): after = lax.ppermute(initial, axis, down)  84.8 us
    ppermute x24, starting transfers between devices, padded_2(): before = lax.ppermute(last, axis, up)  67.5 us
    ppermute x24, starting transfers between devices, padded_2(): after = lax.ppermute(initial, axis, down)  38.7 us
    all_to_all x1, waiting for transfers between devices, shards(): lax.all_to_all(pack_out(old_area), 'curve', split_axis=1, concat_axis=1,...  7.35 us
    all_to_all x1, waiting for transfers between devices, shards(): lax.all_to_all(pack_out(old_volume), 'curve', split_axis=1, concat_axis=1...  5.52 us
    concatenate x24, other arithmetic, padded_2(): value = jnp.concatenate([before, value, after], axis=dim)  5.5 us
    all_to_all x1, starting transfers between devices, shards(): lax.all_to_all(pack_out(old_area), 'curve', split_axis=1, concat_axis=1,...  5.42 us
  transfers between devices with their start and end apart: 51, of which 37 were waited for; matrix products, arithmetic and copies ran while one was open for 2% of the time, Pallas kernels for 0%

commit v1 on v0

v1 whole, which is shorter than its diff:
```python
import functools

import jax
import jax.numpy as jnp
from jax import lax
from jax.experimental import pallas as pl
from jax.experimental.pallas import tpu as pltpu
from jax.sharding import PartitionSpec as P

BS = 32
RB = 4
CB = 8
NCAT = 5
SUB = 6
MOST = 2
SLOT = RB * CB
LANES = 128
ROWS = RB * BS
TILES = CB * BS // LANES
CHUNKS = BS * BS // LANES
PER = LANES // BS
WIDE = 2 * SUB
HALO = 16
TOP = 8
CORE = TOP + HALO
LOW = CORE + ROWS
TALL = LOW + HALO + 8
SPAN = ROWS + 2 * HALO
STEP = 32
FIELDS = 7
MESH = pl.DeviceIdType.MESH


def kernel(
    owners, subs, pairs,
    dyn_ref, area_ref, vol_ref, block_ref, wind_ref, mask_ref,
    vel_ref, stress_ref,
    own, area, vol, send, came, grid, mask, edge, side, source,
    in_sem, out_sem, mig_send, mig_recv, halo_send, halo_recv,
):
    me = lax.axis_index("curve")
    col = lax.axis_index("sub") * pairs + lax.axis_index("pair")
    cols = subs * pairs
    has_up, has_down = me > 0, me < owners - 1
    has_left, has_right = col > 0, col < cols - 1

    def device(d_row, d_col):
        there = lax.rem(col + d_col + cols, cols)
        return {
            "curve": lax.rem(me + d_row + owners, owners),
            "sub": lax.div(there, pairs),
            "pair": lax.rem(there, pairs),
        }

    def exists(d_row, d_col):
        flag = None
        for step, low, high in ((d_row, has_up, has_down), (d_col, has_left, has_right)):
            if step:
                part = low if step < 0 else high
                flag = part if flag is None else jnp.logical_and(flag, part)
        return flag

    loads = []
    for t in range(TILES):
        loads.append(pltpu.make_async_copy(
            wind_ref.at[:, :, pl.ds(t * LANES, LANES)],
            grid.at[pl.ds(FIELDS, 2), t, pl.ds(CORE, ROWS), :], in_sem.at[2 * t]))
        loads.append(pltpu.make_async_copy(
            mask_ref.at[:, pl.ds(t * LANES, LANES)], mask.at[t], in_sem.at[2 * t + 1]))
    base = 2 * TILES
    for j in range(CHUNKS):
        lanes = pl.ds(j * LANES, LANES)
        loads.append(pltpu.make_async_copy(area_ref.at[:, :, lanes], area.at[j], in_sem.at[base + 3 * j]))
        loads.append(pltpu.make_async_copy(vol_ref.at[:, :, lanes], vol.at[j], in_sem.at[base + 3 * j + 1]))
        loads.append(pltpu.make_async_copy(
            dyn_ref.at[:, :, lanes], own.at[j, pl.ds(0, 5)], in_sem.at[base + 3 * j + 2]))
    for load in loads:
        load.start()

    rim = jnp.zeros((10, TILES + 1, CORE, LANES), jnp.float32)
    grid[pl.ds(0, 10), :, pl.ds(0, CORE), :] = rim
    grid[pl.ds(0, 10), :, pl.ds(LOW, CORE), :] = rim
    side[...] = jnp.zeros(side.shape, jnp.float32)

    barrier = pltpu.get_barrier_semaphore()

    def greet(k, carry):
        pl.semaphore_signal(barrier, inc=1, device_id={"curve": lax.rem(me + k, owners)}, device_id_type=MESH)
        return carry

    lax.fori_loop(1, owners, greet, 0)
    count = owners - 1
    around = [(0, -1), (0, 1), (-1, -1), (-1, 1), (1, -1), (1, 1)]
    for d_row, d_col in around:
        flag = exists(d_row, d_col)
        count = count + flag.astype(jnp.int32)

        @pl.when(flag)
        def _():
            pl.semaphore_signal(barrier, inc=1, device_id=device(d_row, d_col), device_id_type=MESH)

    pl.semaphore_wait(barrier, count)

    for load in loads[:base]:
        load.wait()
    grid[9, pl.ds(0, TILES), pl.ds(CORE, ROWS), :] = mask[...].astype(jnp.float32)

    def row_copy(d_row, start, length, slot):
        here = CORE if d_row < 0 else LOW - HALO
        there = LOW if d_row < 0 else TOP
        return pltpu.make_async_remote_copy(
            src_ref=grid.at[pl.ds(start, length), pl.ds(0, TILES), pl.ds(here, HALO), :],
            dst_ref=grid.at[pl.ds(start, length), pl.ds(0, TILES), pl.ds(there, HALO), :],
            send_sem=halo_send.at[slot], recv_sem=halo_recv.at[slot],
            device_id=device(d_row, 0), device_id_type=MESH)

    def each(copies, act):
        for flag, copy in copies:
            @pl.when(flag)
            def _():
                act(copy)

    early = [(exists(-1, 0), row_copy(-1, FIELDS, 3, 0)), (exists(1, 0), row_copy(1, FIELDS, 3, 1))]
    early_back = [(exists(1, 0), early[0][1]), (exists(-1, 0), early[1][1])]
    each(early, lambda copy: copy.start())

    for load in loads[base:]:
        load.wait()

    def derive(j, carry):
        total_area = area[j, 0]
        total_volume = vol[j, 0]
        for n in range(1, NCAT):
            total_area = total_area + area[j, n]
            total_volume = total_volume + vol[j, n]
        own[j, 5] = 2.0 * total_volume * jnp.exp(-2.0 * (1.0 - total_area))
        own[j, 6] = total_volume
        return carry

    lax.fori_loop(0, CHUNKS, derive, 0)

    flat = own.reshape(CHUNKS * FIELDS * SLOT, LANES)

    def block_rows(field, slot):
        return flat[pl.ds(field * SLOT + slot, CHUNKS, stride=FIELDS * SLOT), :]

    def migrate(k):
        to = lax.rem(me + k, owners)
        return pltpu.make_async_remote_copy(
            src_ref=send.at[k], dst_ref=came.at[k],
            send_sem=mig_send.at[k], recv_sem=mig_recv.at[k],
            device_id={"curve": to}, device_id_type=MESH)

    def pack(k, carry):
        to = lax.rem(me + k, owners)
        first, last = jnp.int32(SLOT - 1), jnp.int32(0)
        for s in range(SLOT):
            place = block_ref[me * SLOT + s] - to * SLOT
            match = jnp.logical_and(place >= 0, place < SLOT)
            first = jnp.where(match, jnp.minimum(first, s), first)
            last = jnp.where(match, s, last)
        for rank, slot in enumerate((first, last)):
            for f in range(FIELDS):
                send[k, rank, f] = block_rows(f, slot)
        migrate(k).start()
        return carry

    lax.fori_loop(1, owners, pack, 0)

    for p in range(SLOT):
        source[p] = jnp.int32(-1)

    def find(k, carry):
        giver = lax.rem(me + owners - k, owners)
        rank = jnp.int32(0)
        for p in range(SLOT):
            place = block_ref[giver * SLOT + p] - me * SLOT
            match = jnp.logical_and(place >= 0, place < SLOT)
            source[p] = jnp.where(match, k * MOST + jnp.minimum(rank, MOST - 1), source[p])
            rank = jnp.where(match, rank + 1, rank)
        return carry

    lax.fori_loop(1, owners, find, 0)

    def arrive(k, carry):
        migrate(k).wait_recv()
        return carry

    lax.fori_loop(1, owners, arrive, 0)

    lane = lax.broadcasted_iota(jnp.int32, (CHUNKS, LANES), 1)
    upper = lane >= LANES // 2
    odd = lax.rem(lax.div(lane, BS), 2) == 1
    arrivals = came.reshape(owners * MOST, FIELDS, CHUNKS, LANES)

    def settle(r, carry):
        for h in range(TILES):
            slots = []
            for m in range(PER):
                p = r * CB + h * PER + m
                here = source[p]
                slots.append((p, here >= 0, jnp.maximum(here, MOST)))
            for f in range(FIELDS):
                v0, v1, v2, v3 = [
                    jnp.where(new, arrivals[index, f], block_rows(f, p)) for p, new, index in slots
                ]
                a0 = jnp.where(upper, pltpu.roll(v2, 64, 1), v0)
                a2 = jnp.where(upper, v2, pltpu.roll(v0, 64, 1))
                a1 = jnp.where(upper, pltpu.roll(v3, 64, 1), v1)
                a3 = jnp.where(upper, v3, pltpu.roll(v1, 64, 1))
                rows = (
                    jnp.where(odd, pltpu.roll(a1, 32, 1), a0),
                    jnp.where(odd, a1, pltpu.roll(a0, 96, 1)),
                    jnp.where(odd, pltpu.roll(a3, 32, 1), a2),
                    jnp.where(odd, a3, pltpu.roll(a2, 96, 1)),
                )
                for y, value in enumerate(rows):
                    grid[f, h, pl.ds(CORE + r * BS + y, CHUNKS, stride=PER), :] = value
        return carry

    lax.fori_loop(0, RB, settle, 0)

    late = [(exists(-1, 0), row_copy(-1, 0, FIELDS, 2)), (exists(1, 0), row_copy(1, 0, FIELDS, 3))]
    late_back = [(exists(1, 0), late[0][1]), (exists(-1, 0), late[1][1])]
    each(late, lambda copy: copy.start())

    def strips(i, carry):
        start = pl.multiple_of(i * STEP, 8)
        place = lax.broadcasted_iota(jnp.int32, (STEP, LANES), 1)
        left = jnp.zeros((STEP, LANES), jnp.float32)
        right = jnp.zeros((STEP, LANES), jnp.float32)
        for f in range(10):
            inside = jnp.logical_and(place >= f * WIDE, place < (f + 1) * WIDE)
            first = grid[f, 0, pl.ds(CORE + start, STEP), :]
            last = grid[f, TILES - 1, pl.ds(CORE + start, STEP), :]
            if f:
                first = pltpu.roll(first, f * WIDE, 1)
            left = jnp.where(inside, first, left)
            right = jnp.where(inside, pltpu.roll(last, ((f + 1) * WIDE) % LANES, 1), right)
        edge[0, pl.ds(start, STEP), :] = left
        edge[1, pl.ds(start, STEP), :] = right
        return carry

    lax.fori_loop(0, ROWS // STEP, strips, 0)

    def strip_copy(d_row, d_col, slot):
        which = 0 if d_col < 0 else 1
        here, length, there = {
            0: (0, ROWS, HALO), -1: (0, HALO, HALO + ROWS), 1: (ROWS - HALO, HALO, 0),
        }[d_row]
        return pltpu.make_async_remote_copy(
            src_ref=edge.at[which, pl.ds(here, length), :],
            dst_ref=side.at[which, pl.ds(there, length), :],
            send_sem=halo_send.at[slot], recv_sem=halo_recv.at[slot],
            device_id=device(d_row, d_col), device_id_type=MESH)

    columns, columns_back = [], []
    for i, (d_row, d_col) in enumerate(around):
        copy = strip_copy(d_row, d_col, 4 + i)
        columns.append((exists(d_row, d_col), copy))
        columns_back.append((exists(-d_row, -d_col), copy))
    each(columns, lambda copy: copy.start())
    each(early_back + late_back + columns_back, lambda copy: copy.wait_recv())
    each(early + late + columns, lambda copy: copy.wait_send())

    def spread(i, carry):
        start = pl.multiple_of(i * STEP, 8)
        place = lax.broadcasted_iota(jnp.int32, (STEP, LANES), 1)
        from_right = side[0, pl.ds(start, STEP), :]
        from_left = side[1, pl.ds(start, STEP), :]
        for f in range(10):
            first = pltpu.roll(from_right, (LANES - f * WIDE) % LANES, 1) if f else from_right
            last = pltpu.roll(from_left, LANES - (f + 1) * WIDE, 1)
            grid[f, TILES, pl.ds(TOP + start, STEP), :] = jnp.where(
                place < WIDE, first, jnp.where(place >= LANES - WIDE, last, 0.0))
        for t in range(TILES + 1):
            rows = pl.ds(TOP + start, STEP)
            active = grid[9, t, rows, :]
            strength = grid[5, t, rows, :]
            mass = grid[6, t, rows, :]
            drag = mass + 0.5
            turning = 0.5 * mass
            scale = active / (drag * drag + turning * turning)
            keep = active * (1.0 / 1.5)
            grid[9, t, rows, :] = keep
            grid[5, t, rows, :] = 0.5 * keep * strength
            grid[10, t, rows, :] = scale * drag
            grid[11, t, rows, :] = scale * turning
        return carry

    lax.fori_loop(0, SPAN // STEP, spread, 0)

    all_tiles = range(TILES + 1)
    place = lax.broadcasted_iota(jnp.int32, (STEP, LANES), 1)
    is_first, is_last = place == 0, place == LANES - 1

    def across(values):
        ahead = [pltpu.roll(x, LANES - 1, 1) for x in values]
        behind = [pltpu.roll(x, 1, 1) for x in values]
        n = len(values)
        return [
            jnp.where(is_last, ahead[(t + 1) % n], ahead[t]) - jnp.where(is_first, behind[(t - 1) % n], behind[t])
            for t in range(n)
        ]

    def stress_rows(i, carry):
        start = pl.multiple_of(TOP + i * STEP, 8)
        rows = pl.ds(start, STEP)
        above, below = pl.ds(start - 1, STEP), pl.ds(start + 1, STEP)
        u_x = across([grid[0, t, rows, :] for t in all_tiles])
        v_x = across([grid[1, t, rows, :] for t in all_tiles])
        for t in all_tiles:
            u_y = grid[0, t, below, :] - grid[0, t, above, :]
            v_y = grid[1, t, below, :] - grid[1, t, above, :]
            divergence = u_x[t] + v_y
            tension = u_x[t] - v_y
            shearing = u_y + v_x[t]
            inverse = lax.rsqrt(divergence * divergence + 0.25 * (tension * tension + shearing * shearing) + 1.0)
            keep = grid[9, t, rows, :]
            force = grid[5, t, rows, :]
            scaled = force * inverse
            grid[2, t, rows, :] = keep * grid[2, t, rows, :] + (scaled * divergence - force)
            grid[3, t, rows, :] = keep * grid[3, t, rows, :] + 0.25 * (scaled * tension)
            grid[4, t, rows, :] = keep * grid[4, t, rows, :] + 0.125 * (scaled * shearing)
        return carry

    def velocity_rows(i, carry):
        start = pl.multiple_of(TOP + i * STEP, 8)
        rows = pl.ds(start, STEP)
        above, below = pl.ds(start - 1, STEP), pl.ds(start + 1, STEP)
        sum_x = across([grid[2, t, rows, :] + grid[3, t, rows, :] for t in all_tiles])
        cross_x = across([grid[4, t, rows, :] for t in all_tiles])
        for t in all_tiles:
            cross_y = grid[4, t, below, :] - grid[4, t, above, :]
            lower = grid[2, t, below, :] - grid[3, t, below, :]
            higher = grid[2, t, above, :] - grid[3, t, above, :]
            mass = grid[6, t, rows, :]
            rhs_x = mass * grid[0, t, rows, :] + (0.25 * sum_x[t] + 0.5 * cross_y) + grid[7, t, rows, :]
            rhs_y = mass * grid[1, t, rows, :] + (0.5 * cross_x[t] + 0.25 * (lower - higher)) + grid[8, t, rows, :]
            ahead = grid[10, t, rows, :]
            turn = grid[11, t, rows, :]
            grid[0, t, rows, :] = ahead * rhs_x + turn * rhs_y
            grid[1, t, rows, :] = ahead * rhs_y - turn * rhs_x
        return carry

    def subcycle(n, carry):
        lax.fori_loop(0, SPAN // STEP, stress_rows, 0)
        lax.fori_loop(0, SPAN // STEP, velocity_rows, 0)
        return carry

    lax.fori_loop(0, SUB, subcycle, 0)

    stores = []
    for t in range(TILES):
        lanes = pl.ds(t * LANES, LANES)
        stores.append(pltpu.make_async_copy(
            grid.at[pl.ds(0, 2), t, pl.ds(CORE, ROWS), :], vel_ref.at[:, :, lanes], out_sem.at[2 * t]))
        stores.append(pltpu.make_async_copy(
            grid.at[pl.ds(2, 3), t, pl.ds(CORE, ROWS), :], stress_ref.at[:, :, lanes], out_sem.at[2 * t + 1]))
    for store in stores:
        store.start()

    def sent(k, carry):
        migrate(k).wait_send()
        return carry

    lax.fori_loop(1, owners, sent, 0)
    for store in stores:
        store.wait()


def shards(old_dynamics, old_area, old_volume, old_block, wind_stress, ice_mask):
    owners, subs, pairs = (lax.axis_size(name) for name in ("curve", "sub", "pair"))
    anywhere = pl.BlockSpec(memory_space=pl.ANY)
    real = jnp.float32
    return pl.pallas_call(
        functools.partial(kernel, owners, subs, pairs),
        out_shape=(
            jax.ShapeDtypeStruct((2, ROWS, CB * BS), real),
            jax.ShapeDtypeStruct((3, ROWS, CB * BS), real),
        ),
        in_specs=[anywhere] * 3 + [pl.BlockSpec(memory_space=pltpu.SMEM)] + [anywhere] * 2,
        out_specs=(anywhere, anywhere),
        scratch_shapes=[
            pltpu.VMEM((CHUNKS, FIELDS, SLOT, LANES), real),
            pltpu.VMEM((CHUNKS, NCAT, SLOT, LANES), real),
            pltpu.VMEM((CHUNKS, NCAT, SLOT, LANES), real),
            pltpu.VMEM((owners, MOST, FIELDS, CHUNKS, LANES), real),
            pltpu.VMEM((owners, MOST, FIELDS, CHUNKS, LANES), real),
            pltpu.VMEM((12, TILES + 1, TALL, LANES), real),
            pltpu.VMEM((TILES, ROWS, LANES), jnp.int32),
            pltpu.VMEM((2, ROWS, LANES), real),
            pltpu.VMEM((2, SPAN, LANES), real),
            pltpu.SMEM((SLOT,), jnp.int32),
            pltpu.SemaphoreType.DMA((2 * TILES + 3 * CHUNKS,)),
            pltpu.SemaphoreType.DMA((2 * TILES,)),
            pltpu.SemaphoreType.DMA((owners,)),
            pltpu.SemaphoreType.DMA((owners,)),
            pltpu.SemaphoreType.DMA((10,)),
            pltpu.SemaphoreType.DMA((10,)),
        ],
        compiler_params=pltpu.CompilerParams(
            collective_id=0, has_side_effects=True, vmem_limit_bytes=40 * 1024 * 1024
        ),
    )(old_dynamics, old_area, old_volume, old_block, wind_stress, ice_mask)


def solution(mesh):
    return jax.shard_map(
        shards,
        mesh=mesh,
        in_specs=(
            P("groups", "curve", ("sub", "pair")),
            P("groups", "curve", ("sub", "pair")),
            P("groups", "curve", ("sub", "pair")),
            P(),
            P(None, ("groups", "curve"), ("sub", "pair")),
            P(("groups", "curve"), ("sub", "pair")),
        ),
        out_specs=(
            P(None, ("groups", "curve"), ("sub", "pair")),
            P(None, ("groups", "curve"), ("sub", "pair")),
        ),
        check_vma=False,
    )
```

time: 267 us -> 37.4 us (0.14)
  starting transfers between devices: 118 us -> 0 us
  waiting for transfers between devices: 106 us -> 0 us
  Pallas kernels: 0 us -> 28.8 us
  other arithmetic: 18.6 us -> 0 us
  local copies, waits for them, and re-layouts: 20.2 us -> 7.21 us
    ppermute x48 -> x0, starting transfers between devices: 106 us -> none  [the longest x24 67.5 us: padded_2(): before = lax.ppermute(last, axis, up)]
    ppermute x48 -> x0, waiting for transfers between devices: 89.1 us -> none  [the longest x24 84.8 us: padded_2(): after = lax.ppermute(initial, axis, down)]
    pallas_call x0 -> x1, Pallas kernels: none -> 28.8 us  [shards(): pl.pallas_call(functools.partial(kernel, owners, subs, pairs), out_shape=...]
    all_to_all x3 -> x0, waiting for transfers between devices: 17.2 us -> none  [the longest x1 7.35 us: shards(): lax.all_to_all(pack_out(old_area), 'curve', split_axis=1, concat_axis=1,...]
    all_to_all x3 -> x0, starting transfers between devices: 12.2 us -> none  [the longest x1 5.42 us: shards(): lax.all_to_all(pack_out(old_area), 'curve', split_axis=1, concat_axis=1,...]
    slice x26 -> x0, local copies, waits for them, and re-layouts: 7.71 us -> none  [the longest x3 2 us: shards(): velocity = dynamics[0:2]]
    concatenate x24 -> x0, other arithmetic: 5.5 us -> none  [padded_2(): value = jnp.concatenate([before, value, after], axis=dim)]
    gather x6 -> x0, local copies, waits for them, and re-layouts: 4.51 us -> none  [the longest x3 2.81 us: place_in(): jnp.take(came, source_pos, axis=1)]
  transfers between devices with their start and end apart: 51 -> 0, of which waited for: 37 -> 0; matrix products, arithmetic and copies ran while one was open for 2% -> 0% of each run, Pallas kernels for 0% -> 0%
where the time goes in v1:
time: 37.4 us; the launch traced here: 36.7 us
  Pallas kernels  28.8 us (77%)
  local copies, waits for them, and re-layouts  7.21 us (19%)
  between operations  0.65 us (2%)
    pallas_call x1, Pallas kernels, shards(): pl.pallas_call(functools.partial(kernel, owners, subs, pairs), out_shape=...  28.8 us
    unnamed x14, local copies, waits for them, and re-layouts  7.21 us

profile of v1, /device:TPU:1, one launch (start us, length us, event | category | flops | bytes accessed | tf_op | source)
XLA Modules:
  0.0 36.7 jit_solution(15601893301584918225)
XLA Ops:
  0.6 0.0 copy-start
  0.6 1.1 %copy-done = f32[5,32,1024]{2,1,0:T(8,128)S(1)} copy-done((f32[5,32,1024]{2,1,0:T(8,128)S(1)}, f32[5,32,1024]{2,1,0:T(8,128)}, u32[]{:S(2)}) %copy-start) | copy-done | bytes 655384
  1.7 0.0 copy-start.1
  1.7 1.1 %copy-done.1 = f32[5,32,1024]{2,1,0:T(8,128)S(1)} copy-done((f32[5,32,1024]{2,1,0:T(8,128)S(1)}, f32[5,32,1024]{2,1,0:T(8,128)}, u32[]{:S(2)}) %copy-start.1) | copy-done | bytes 655384
  2.8 0.0 copy-start.2
  2.8 1.1 %copy-done.2 = f32[5,32,1024]{2,1,0:T(8,128)S(1)} copy-done((f32[5,32,1024]{2,1,0:T(8,128)S(1)}, f32[5,32,1024]{2,1,0:T(8,128)}, u32[]{:S(2)}) %copy-start.2) | copy-done | bytes 655384
  3.9 0.0 copy-start.3
  3.9 0.9 %copy-done.3 = f32[2,128,256]{2,1,0:T(8,128)S(1)} copy-done((f32[2,128,256]{2,1,0:T(8,128)S(1)}, f32[2,128,256]{2,1,0:T(8,128)}, u32[]{:S(2)}) %copy-start.3) | copy-done | bytes 262168
  4.8 0.0 copy-start.4
  4.8 0.9 %copy-done.4 = s32[128,256]{1,0:T(8,128)S(1)} copy-done((s32[128,256]{1,0:T(8,128)S(1)}, s32[128,256]{1,0:T(8,128)}, u32[]{:S(2)}) %copy-start.4) | copy-done | bytes 131096
  5.8 0.0 copy-start.5
  5.8 0.7 %copy-done.5 = s32[128]{0:T(128)S(1)} copy-done((s32[128]{0:T(128)S(1)}, s32[128]{0:T(128)}, u32[]{:S(2)}) %copy-start.5) | copy-done | bytes 536
  6.4 28.8 %shard_map.77 = (f32[2,128,256]{2,1,0:T(8,128)S(1)}, f32[3,128,256]{2,1,0:T(8,128)S(1)}) custom-call(f32[5,32,1024]{2,1,0:T(8,128)S(1)} %copy-done, f32[5,32,1024]{2,1,0:T(8,128)S(1)} %copy-done.1, f32[5,32,1024]{2,1,0:T(8,128)S(1)} %copy-done.2, s32[128]{0:T(128)S(1)} %copy-done.5, f32[2,128,256]{2,1,0:T(8,128)S(1)} %copy-done.3, s32[128,256]{1,0:T(8,128)S(1)} %copy-done.4), custom_call_target="tpu_custom_call" | custom-call | tf_op jit(solution)/shard_map/pallas_call | solution.py:376
  35.3 0.7 %copy.10 = f32[2,128,256]{2,1,0:T(8,128)} copy(f32[2,128,256]{2,1,0:T(8,128)S(1)} %get-tuple-element.4) | data formatting | bytes 524288
  36.0 0.7 %copy.11 = f32[3,128,256]{2,1,0:T(8,128)} copy(f32[3,128,256]{2,1,0:T(8,128)S(1)} %get-tuple-element.5) | data formatting | bytes 786432
Async XLA Ops:
  0.6 1.1 %copy-start = (f32[5,32,1024]{2,1,0:T(8,128)S(1)}, f32[5,32,1024]{2,1,0:T(8,128)}, u32[]{:S(2)}) copy-start(f32[5,32,1024]{2,1,0:T(8,128)} %dyn_ref.1) | copy-start | bytes 1966084
  1.7 1.1 %copy-start.1 = (f32[5,32,1024]{2,1,0:T(8,128)S(1)}, f32[5,32,1024]{2,1,0:T(8,128)}, u32[]{:S(2)}) copy-start(f32[5,32,1024]{2,1,0:T(8,128)} %area_ref.1) | copy-start | bytes 1966084
  2.8 1.1 %copy-start.2 = (f32[5,32,1024]{2,1,0:T(8,128)S(1)}, f32[5,32,1024]{2,1,0:T(8,128)}, u32[]{:S(2)}) copy-start(f32[5,32,1024]{2,1,0:T(8,128)} %vol_ref.1) | copy-start | bytes 1966084
  3.9 0.9 %copy-start.3 = (f32[2,128,256]{2,1,0:T(8,128)S(1)}, f32[2,128,256]{2,1,0:T(8,128)}, u32[]{:S(2)}) copy-start(f32[2,128,256]{2,1,0:T(8,128)} %wind_ref.1) | copy-start | bytes 786436
  4.8 0.9 %copy-start.4 = (s32[128,256]{1,0:T(8,128)S(1)}, s32[128,256]{1,0:T(8,128)}, u32[]{:S(2)}) copy-start(s32[128,256]{1,0:T(8,128)} %mask_ref.1) | copy-start | bytes 393220
  5.8 0.7 %copy-start.5 = (s32[128]{0:T(128)S(1)}, s32[128]{0:T(128)}, u32[]{:S(2)}) copy-start(s32[128]{0:T(128)} %block_ref.1) | copy-start | bytes 1540

commit v2 on v1

--- a/solution.py
+++ b/solution.py
@@ -27,6 +27,9 @@
 TALL = LOW + HALO + 8
 SPAN = ROWS + 2 * HALO
 STEP = 32
+PIECE = 16
+UNROLL = True
+LIMIT = 56
 FIELDS = 7
 MESH = pl.DeviceIdType.MESH
 
@@ -34,8 +37,8 @@
 def kernel(
     owners, subs, pairs,
     dyn_ref, area_ref, vol_ref, block_ref, wind_ref, mask_ref,
-    vel_ref, stress_ref,
-    own, area, vol, send, came, grid, mask, edge, side, source,
+    vel_out, stress_out,
+    vel_ref, stress_ref, fixed_ref, final, own, area, vol, send, came, grid, mask, edge, side, source,
     in_sem, out_sem, mig_send, mig_recv, halo_send, halo_recv,
 ):
     me = lax.axis_index("curve")
@@ -77,9 +80,13 @@
     for load in loads:
         load.start()
 
-    rim = jnp.zeros((10, TILES + 1, CORE, LANES), jnp.float32)
-    grid[pl.ds(0, 10), :, pl.ds(0, CORE), :] = rim
-    grid[pl.ds(0, 10), :, pl.ds(LOW, CORE), :] = rim
+    rim = jnp.zeros((10, TILES, CORE, LANES), jnp.float32)
+    grid[:, :, pl.ds(0, CORE), :] = rim
+    grid[:, :, pl.ds(LOW, CORE), :] = rim
+    for ref in (vel_ref, stress_ref):
+        pad = jnp.zeros((ref.shape[0], TILES + 1, TOP, LANES), jnp.float32)
+        ref[:, :, pl.ds(0, TOP), :] = pad
+        ref[:, :, pl.ds(TALL - TOP, TOP), :] = pad
     side[...] = jnp.zeros(side.shape, jnp.float32)
 
     barrier = pltpu.get_barrier_semaphore()
@@ -261,37 +268,54 @@
         columns_back.append((exists(-d_row, -d_col), copy))
     each(columns, lambda copy: copy.start())
     each(early_back + late_back + columns_back, lambda copy: copy.wait_recv())
-    each(early + late + columns, lambda copy: copy.wait_send())
 
     def spread(i, carry):
         start = pl.multiple_of(i * STEP, 8)
         place = lax.broadcasted_iota(jnp.int32, (STEP, LANES), 1)
         from_right = side[0, pl.ds(start, STEP), :]
         from_left = side[1, pl.ds(start, STEP), :]
+        rows = pl.ds(TOP + start, STEP)
+        values = []
         for f in range(10):
             first = pltpu.roll(from_right, (LANES - f * WIDE) % LANES, 1) if f else from_right
             last = pltpu.roll(from_left, LANES - (f + 1) * WIDE, 1)
-            grid[f, TILES, pl.ds(TOP + start, STEP), :] = jnp.where(
-                place < WIDE, first, jnp.where(place >= LANES - WIDE, last, 0.0))
+            beyond = jnp.where(place < WIDE, first, jnp.where(place >= LANES - WIDE, last, 0.0))
+            values.append([grid[f, t, rows, :] for t in range(TILES)] + [beyond])
         for t in range(TILES + 1):
-            rows = pl.ds(TOP + start, STEP)
-            active = grid[9, t, rows, :]
-            strength = grid[5, t, rows, :]
-            mass = grid[6, t, rows, :]
+            u, v, s1, s2, s12, strength, mass, wind_x, wind_y, active = [value[t] for value in values]
             drag = mass + 0.5
             turning = 0.5 * mass
             scale = active / (drag * drag + turning * turning)
             keep = active * (1.0 / 1.5)
-            grid[9, t, rows, :] = keep
-            grid[5, t, rows, :] = 0.5 * keep * strength
-            grid[10, t, rows, :] = scale * drag
-            grid[11, t, rows, :] = scale * turning
+            vel_ref[0, t, rows, :] = u
+            vel_ref[1, t, rows, :] = v
+            stress_ref[0, t, rows, :] = 0.25 * s1
+            stress_ref[1, t, rows, :] = 0.25 * s2
+            stress_ref[2, t, rows, :] = 0.5 * s12
+            fixed_ref[0, t, rows, :] = keep
+            fixed_ref[1, t, rows, :] = 0.125 * keep * strength
+            fixed_ref[2, t, rows, :] = mass
+            fixed_ref[3, t, rows, :] = wind_x
+            fixed_ref[4, t, rows, :] = wind_y
+            fixed_ref[5, t, rows, :] = scale * drag
+            fixed_ref[6, t, rows, :] = scale * turning
         return carry
 
     lax.fori_loop(0, SPAN // STEP, spread, 0)
 
-    all_tiles = range(TILES + 1)
-    place = lax.broadcasted_iota(jnp.int32, (STEP, LANES), 1)
+    cycles(vel_out, stress_out, vel_ref, stress_ref, fixed_ref, final, out_sem)
+
+    def sent(k, carry):
+        migrate(k).wait_send()
+        return carry
+
+    lax.fori_loop(1, owners, sent, 0)
+    each(early + late + columns, lambda copy: copy.wait_send())
+
+
+def cycles(vel_out, stress_out, vel, stress, fixed, final, out_sem):
+    tiles = range(TILES + 1)
+    place = lax.broadcasted_iota(jnp.int32, (PIECE, LANES), 1)
     is_first, is_last = place == 0, place == LANES - 1
 
     def across(values):
@@ -303,68 +327,88 @@
             for t in range(n)
         ]
 
-    def stress_rows(i, carry):
-        start = pl.multiple_of(TOP + i * STEP, 8)
-        rows = pl.ds(start, STEP)
-        above, below = pl.ds(start - 1, STEP), pl.ds(start + 1, STEP)
-        u_x = across([grid[0, t, rows, :] for t in all_tiles])
-        v_x = across([grid[1, t, rows, :] for t in all_tiles])
-        for t in all_tiles:
-            u_y = grid[0, t, below, :] - grid[0, t, above, :]
-            v_y = grid[1, t, below, :] - grid[1, t, above, :]
-            divergence = u_x[t] + v_y
-            tension = u_x[t] - v_y
-            shearing = u_y + v_x[t]
-            inverse = lax.rsqrt(divergence * divergence + 0.25 * (tension * tension + shearing * shearing) + 1.0)
-            keep = grid[9, t, rows, :]
-            force = grid[5, t, rows, :]
-            scaled = force * inverse
-            grid[2, t, rows, :] = keep * grid[2, t, rows, :] + (scaled * divergence - force)
-            grid[3, t, rows, :] = keep * grid[3, t, rows, :] + 0.25 * (scaled * tension)
-            grid[4, t, rows, :] = keep * grid[4, t, rows, :] + 0.125 * (scaled * shearing)
-        return carry
-
-    def velocity_rows(i, carry):
-        start = pl.multiple_of(TOP + i * STEP, 8)
-        rows = pl.ds(start, STEP)
-        above, below = pl.ds(start - 1, STEP), pl.ds(start + 1, STEP)
-        sum_x = across([grid[2, t, rows, :] + grid[3, t, rows, :] for t in all_tiles])
-        cross_x = across([grid[4, t, rows, :] for t in all_tiles])
-        for t in all_tiles:
-            cross_y = grid[4, t, below, :] - grid[4, t, above, :]
-            lower = grid[2, t, below, :] - grid[3, t, below, :]
-            higher = grid[2, t, above, :] - grid[3, t, above, :]
-            mass = grid[6, t, rows, :]
-            rhs_x = mass * grid[0, t, rows, :] + (0.25 * sum_x[t] + 0.5 * cross_y) + grid[7, t, rows, :]
-            rhs_y = mass * grid[1, t, rows, :] + (0.5 * cross_x[t] + 0.25 * (lower - higher)) + grid[8, t, rows, :]
-            ahead = grid[10, t, rows, :]
-            turn = grid[11, t, rows, :]
-            grid[0, t, rows, :] = ahead * rhs_x + turn * rhs_y
-            grid[1, t, rows, :] = ahead * rhs_y - turn * rhs_x
-        return carry
-
-    def subcycle(n, carry):
-        lax.fori_loop(0, SPAN // STEP, stress_rows, 0)
-        lax.fori_loop(0, SPAN // STEP, velocity_rows, 0)
-        return carry
-
-    lax.fori_loop(0, SUB, subcycle, 0)
-
+    def update_stress(vel_in, stress_in, first_row, pieces):
+        def body(i, carry):
+            start = pl.multiple_of(first_row + i * PIECE, 8)
+            rows, above, below = (pl.ds(start + d, PIECE) for d in (0, -1, 1))
+            u_x = across([vel_in[0, t, rows, :] for t in tiles])
+            v_x = across([vel_in[1, t, rows, :] for t in tiles])
+            results = []
+            for t in tiles:
+                u_y = vel_in[0, t, below, :] - vel_in[0, t, above, :]
+                v_y = vel_in[1, t, below, :] - vel_in[1, t, above, :]
+                divergence = u_x[t] + v_y
+                tension = u_x[t] - v_y
+                shearing = u_y + v_x[t]
+                inverse = lax.rsqrt(divergence * divergence + 0.25 * (tension * tension + shearing * shearing) + 1.0)
+                keep = fixed[0, t, rows, :]
+                force = fixed[1, t, rows, :]
+                scaled = force * inverse
+                quarter = 0.25 * scaled
+                results.append((
+                    keep * stress_in[0, t, rows, :] + (scaled * divergence - force),
+                    keep * stress_in[1, t, rows, :] + quarter * tension,
+                    keep * stress_in[2, t, rows, :] + quarter * shearing,
+                ))
+            for t in tiles:
+                for f in range(3):
+                    stress[f, t, rows, :] = results[t][f]
+            return carry
+
+        lax.fori_loop(0, pieces, body, 0, unroll=UNROLL)
+
+    def update_velocity(vel_in, first_row, pieces):
+        def body(i, carry):
+            start = pl.multiple_of(first_row + i * PIECE, 8)
+            rows, above, below = (pl.ds(start + d, PIECE) for d in (0, -1, 1))
+            sum_x = across([stress[0, t, rows, :] + stress[1, t, rows, :] for t in tiles])
+            cross_x = across([stress[2, t, rows, :] for t in tiles])
+            results = []
+            for t in tiles:
+                cross_y = stress[2, t, below, :] - stress[2, t, above, :]
+                lower = stress[0, t, below, :] - stress[1, t, below, :]
+                higher = stress[0, t, above, :] - stress[1, t, above, :]
+                mass = fixed[2, t, rows, :]
+                rhs_x = mass * vel_in[0, t, rows, :] + (sum_x[t] + cross_y) + fixed[3, t, rows, :]
+                rhs_y = mass * vel_in[1, t, rows, :] + (cross_x[t] + (lower - higher)) + fixed[4, t, rows, :]
+                ahead = fixed[5, t, rows, :]
+                turn = fixed[6, t, rows, :]
+                results.append((ahead * rhs_x + turn * rhs_y, ahead * rhs_y - turn * rhs_x))
+            for t in tiles:
+                for f in range(2):
+                    vel[f, t, rows, :] = results[t][f]
+            return carry
+
+        lax.fori_loop(0, pieces, body, 0, unroll=UNROLL)
+
+    wide, middle = [(CORE - out, (ROWS + 2 * out) // PIECE) for out in (HALO, HALO // 2)]
     stores = []
     for t in range(TILES):
-        lanes = pl.ds(t * LANES, LANES)
         stores.append(pltpu.make_async_copy(
-            grid.at[pl.ds(0, 2), t, pl.ds(CORE, ROWS), :], vel_ref.at[:, :, lanes], out_sem.at[2 * t]))
+            final.at[:, t], stress_out.at[:, :, pl.ds(t * LANES, LANES)], out_sem.at[t]))
+    for t in range(TILES):
         stores.append(pltpu.make_async_copy(
-            grid.at[pl.ds(2, 3), t, pl.ds(CORE, ROWS), :], stress_ref.at[:, :, lanes], out_sem.at[2 * t + 1]))
-    for store in stores:
+            vel.at[:, t, pl.ds(CORE, ROWS), :], vel_out.at[:, :, pl.ds(t * LANES, LANES)],
+            out_sem.at[TILES + t]))
+
+    def early(n, carry):
+        update_stress(vel, stress, *wide)
+        update_velocity(vel, *wide)
+        return carry
+
+    def subcycle(n, carry):
+        update_stress(vel, stress, *middle)
+        update_velocity(vel, *middle)
+        return carry
+
+    lax.fori_loop(0, 2, early, 0)
+    lax.fori_loop(2, SUB, subcycle, 0)
+    for store in stores[TILES:]:
         store.start()
-
-    def sent(k, carry):
-        migrate(k).wait_send()
-        return carry
-
-    lax.fori_loop(1, owners, sent, 0)
+    for t in range(TILES):
+        for f, factor in enumerate((4.0, 4.0, 2.0)):
+            final[f, t] = factor * stress[f, t, pl.ds(CORE, ROWS), :]
+        stores[t].start()
     for store in stores:
         store.wait()
 
@@ -382,12 +426,16 @@
         in_specs=[anywhere] * 3 + [pl.BlockSpec(memory_space=pltpu.SMEM)] + [anywhere] * 2,
         out_specs=(anywhere, anywhere),
         scratch_shapes=[
+            pltpu.VMEM((2, TILES + 1, TALL, LANES), real),
+            pltpu.VMEM((3, TILES + 1, TALL, LANES), real),
+            pltpu.VMEM((7, TILES + 1, TALL, LANES), real),
+            pltpu.VMEM((3, TILES, ROWS, LANES), real),
             pltpu.VMEM((CHUNKS, FIELDS, SLOT, LANES), real),
             pltpu.VMEM((CHUNKS, NCAT, SLOT, LANES), real),
             pltpu.VMEM((CHUNKS, NCAT, SLOT, LANES), real),
             pltpu.VMEM((owners, MOST, FIELDS, CHUNKS, LANES), real),
             pltpu.VMEM((owners, MOST, FIELDS, CHUNKS, LANES), real),
-            pltpu.VMEM((12, TILES + 1, TALL, LANES), real),
+            pltpu.VMEM((10, TILES, TALL, LANES), real),
             pltpu.VMEM((TILES, ROWS, LANES), jnp.int32),
             pltpu.VMEM((2, ROWS, LANES), real),
             pltpu.VMEM((2, SPAN, LANES), real),
@@ -400,7 +448,7 @@
             pltpu.SemaphoreType.DMA((10,)),
         ],
         compiler_params=pltpu.CompilerParams(
-            collective_id=0, has_side_effects=True, vmem_limit_bytes=40 * 1024 * 1024
+            collective_id=0, has_side_effects=True, vmem_limit_bytes=LIMIT * 1024 * 1024
         ),
     )(old_dynamics, old_area, old_volume, old_block, wind_stress, ice_mask)
 

time: 37.4 us -> 28 us (0.75)
  local copies, waits for them, and re-layouts: 7.21 us -> 2.47 us
  Pallas kernels: 28.8 us -> 24.4 us
    unnamed x14 -> x4, local copies, waits for them, and re-layouts: 7.21 us -> 2.47 us
    pallas_call x1, Pallas kernels: 28.8 us -> 24.4 us  [shards(): pl.pallas_call(functools.partial(kernel, owners, subs, pairs), out_shape=...]
where the time goes in v2:
time: 28 us; the launch traced here: 27.6 us
  Pallas kernels  24.4 us (87%)
  local copies, waits for them, and re-layouts  2.47 us (9%)
  between operations  0.65 us (2%)
    pallas_call x1, Pallas kernels, shards(): pl.pallas_call(functools.partial(kernel, owners, subs, pairs), out_shape=...  24.4 us
    unnamed x4, local copies, waits for them, and re-layouts  2.47 us

profile of v2, /device:TPU:1, one launch (start us, length us, event | category | flops | bytes accessed | tf_op | source)
XLA Modules:
  0.0 27.6 jit_solution(10233804243749677113)
XLA Ops:
  0.6 24.4 %shard_map.77 = (f32[2,128,256]{2,1,0:T(8,128)}, f32[3,128,256]{2,1,0:T(8,128)}) custom-call(f32[5,32,1024]{2,1,0:T(8,128)} %dyn_ref.1, f32[5,32,1024]{2,1,0:T(8,128)} %area_ref.1, f32[5,32,1024]{2,1,0:T(8,128)} %vol_ref.1, s32[128]{0:T(128)} %block_ref.1, f32[2,128,256]{2,1,0:T(8,128)} %wind_ref.1, s32[128,256]{1,0:T(8,128)} %mask_ref.1), custom_call_target="tpu_custom_call" | custom-call | tf_op jit(solution)/shard_map/pallas_call | solution.py:420
  25.1 0.0 copy-start
  25.1 1.7 %copy.10 = f32[2,128,256]{2,1,0:T(8,128)} copy(f32[2,128,256]{2,1,0:T(8,128)} %get-tuple-element.4) | data formatting | bytes 524288
  26.8 0.0 copy-done
  26.8 0.7 %copy.11 = f32[3,128,256]{2,1,0:T(8,128)} copy(f32[3,128,256]{2,1,0:T(8,128)S(1)} %copy-done) | data formatting | bytes 786432
Async XLA Ops:
  25.1 1.7 %copy-start = (f32[3,128,256]{2,1,0:T(8,128)S(1)}, f32[3,128,256]{2,1,0:T(8,128)}, u32[]{:S(2)}) copy-start(f32[3,128,256]{2,1,0:T(8,128)} %get-tuple-element.5) | copy-start | bytes 1179652

commit v3 on v2

--- a/solution.py
+++ b/solution.py
@@ -21,6 +21,7 @@
 PER = LANES // BS
 WIDE = 2 * SUB
 HALO = 16
+DEEP = 12
 TOP = 8
 CORE = TOP + HALO
 LOW = CORE + ROWS
@@ -106,31 +107,6 @@
         def _():
             pl.semaphore_signal(barrier, inc=1, device_id=device(d_row, d_col), device_id_type=MESH)
 
-    pl.semaphore_wait(barrier, count)
-
-    for load in loads[:base]:
-        load.wait()
-    grid[9, pl.ds(0, TILES), pl.ds(CORE, ROWS), :] = mask[...].astype(jnp.float32)
-
-    def row_copy(d_row, start, length, slot):
-        here = CORE if d_row < 0 else LOW - HALO
-        there = LOW if d_row < 0 else TOP
-        return pltpu.make_async_remote_copy(
-            src_ref=grid.at[pl.ds(start, length), pl.ds(0, TILES), pl.ds(here, HALO), :],
-            dst_ref=grid.at[pl.ds(start, length), pl.ds(0, TILES), pl.ds(there, HALO), :],
-            send_sem=halo_send.at[slot], recv_sem=halo_recv.at[slot],
-            device_id=device(d_row, 0), device_id_type=MESH)
-
-    def each(copies, act):
-        for flag, copy in copies:
-            @pl.when(flag)
-            def _():
-                act(copy)
-
-    early = [(exists(-1, 0), row_copy(-1, FIELDS, 3, 0)), (exists(1, 0), row_copy(1, FIELDS, 3, 1))]
-    early_back = [(exists(1, 0), early[0][1]), (exists(-1, 0), early[1][1])]
-    each(early, lambda copy: copy.start())
-
     for load in loads[base:]:
         load.wait()
 
@@ -169,10 +145,39 @@
         for rank, slot in enumerate((first, last)):
             for f in range(FIELDS):
                 send[k, rank, f] = block_rows(f, slot)
+        return carry
+
+    lax.fori_loop(1, owners, pack, 0)
+    pl.semaphore_wait(barrier, count)
+
+    def depart(k, carry):
         migrate(k).start()
         return carry
 
-    lax.fori_loop(1, owners, pack, 0)
+    lax.fori_loop(1, owners, depart, 0)
+
+    for load in loads[:base]:
+        load.wait()
+    grid[9, pl.ds(0, TILES), pl.ds(CORE, ROWS), :] = mask[...].astype(jnp.float32)
+
+    def row_copy(d_row, start, length, slot):
+        here = CORE if d_row < 0 else LOW - DEEP
+        there = LOW if d_row < 0 else CORE - DEEP
+        return pltpu.make_async_remote_copy(
+            src_ref=grid.at[pl.ds(start, length), pl.ds(0, TILES), pl.ds(here, DEEP), :],
+            dst_ref=grid.at[pl.ds(start, length), pl.ds(0, TILES), pl.ds(there, DEEP), :],
+            send_sem=halo_send.at[slot], recv_sem=halo_recv.at[slot],
+            device_id=device(d_row, 0), device_id_type=MESH)
+
+    def each(copies, act):
+        for flag, copy in copies:
+            @pl.when(flag)
+            def _():
+                act(copy)
+
+    early = [(exists(-1, 0), row_copy(-1, FIELDS, 3, 0)), (exists(1, 0), row_copy(1, FIELDS, 3, 1))]
+    early_back = [(exists(1, 0), early[0][1]), (exists(-1, 0), early[1][1])]
+    each(early, lambda copy: copy.start())
 
     for p in range(SLOT):
         source[p] = jnp.int32(-1)
@@ -253,7 +258,7 @@
     def strip_copy(d_row, d_col, slot):
         which = 0 if d_col < 0 else 1
         here, length, there = {
-            0: (0, ROWS, HALO), -1: (0, HALO, HALO + ROWS), 1: (ROWS - HALO, HALO, 0),
+            0: (0, ROWS, HALO), -1: (0, DEEP, HALO + ROWS), 1: (ROWS - DEEP, DEEP, HALO - DEEP),
         }[d_row]
         return pltpu.make_async_remote_copy(
             src_ref=edge.at[which, pl.ds(here, length), :],
@@ -267,7 +272,37 @@
         columns.append((exists(d_row, d_col), copy))
         columns_back.append((exists(-d_row, -d_col), copy))
     each(columns, lambda copy: copy.start())
+    def prepare(t, rows, values):
+        u, v, s1, s2, s12, strength, mass, wind_x, wind_y, active = values
+        drag = mass + 0.5
+        turning = 0.5 * mass
+        scale = active / (drag * drag + turning * turning)
+        keep = active * (1.0 / 1.5)
+        vel_ref[0, t, rows, :] = u
+        vel_ref[1, t, rows, :] = v
+        stress_ref[0, t, rows, :] = 0.25 * s1
+        stress_ref[1, t, rows, :] = 0.25 * s2
+        stress_ref[2, t, rows, :] = 0.5 * s12
+        fixed_ref[0, t, rows, :] = keep
+        fixed_ref[1, t, rows, :] = 0.125 * keep * strength
+        fixed_ref[2, t, rows, :] = mass
+        fixed_ref[3, t, rows, :] = wind_x
+        fixed_ref[4, t, rows, :] = wind_y
+        fixed_ref[5, t, rows, :] = scale * drag
+        fixed_ref[6, t, rows, :] = scale * turning
+
+    def interior(i, carry):
+        rows = pl.ds(pl.multiple_of(CORE + i * STEP, 8), STEP)
+        for t in range(TILES):
+            prepare(t, rows, [grid[f, t, rows, :] for f in range(10)])
+        return carry
+
+    lax.fori_loop(0, ROWS // STEP, interior, 0)
     each(early_back + late_back + columns_back, lambda copy: copy.wait_recv())
+    for t in range(TILES):
+        for start in (TOP, LOW):
+            rows = pl.ds(start, HALO)
+            prepare(t, rows, [grid[f, t, rows, :] for f in range(10)])
 
     def spread(i, carry):
         start = pl.multiple_of(i * STEP, 8)
@@ -280,25 +315,8 @@
             first = pltpu.roll(from_right, (LANES - f * WIDE) % LANES, 1) if f else from_right
             last = pltpu.roll(from_left, LANES - (f + 1) * WIDE, 1)
             beyond = jnp.where(place < WIDE, first, jnp.where(place >= LANES - WIDE, last, 0.0))
-            values.append([grid[f, t, rows, :] for t in range(TILES)] + [beyond])
-        for t in range(TILES + 1):
-            u, v, s1, s2, s12, strength, mass, wind_x, wind_y, active = [value[t] for value in values]
-            drag = mass + 0.5
-            turning = 0.5 * mass
-            scale = active / (drag * drag + turning * turning)
-            keep = active * (1.0 / 1.5)
-            vel_ref[0, t, rows, :] = u
-            vel_ref[1, t, rows, :] = v
-            stress_ref[0, t, rows, :] = 0.25 * s1
-            stress_ref[1, t, rows, :] = 0.25 * s2
-            stress_ref[2, t, rows, :] = 0.5 * s12
-            fixed_ref[0, t, rows, :] = keep
-            fixed_ref[1, t, rows, :] = 0.125 * keep * strength
-            fixed_ref[2, t, rows, :] = mass
-            fixed_ref[3, t, rows, :] = wind_x
-            fixed_ref[4, t, rows, :] = wind_y
-            fixed_ref[5, t, rows, :] = scale * drag
-            fixed_ref[6, t, rows, :] = scale * turning
+            values.append(beyond)
+        prepare(TILES, rows, values)
         return carry
 
     lax.fori_loop(0, SPAN // STEP, spread, 0)

time: 28 us -> 26.8 us (0.957)
  Pallas kernels: 24.4 us -> 23.4 us
    pallas_call x1, Pallas kernels: 24.4 us -> 23.4 us  [shards(): pl.pallas_call(functools.partial(kernel, owners, subs, pairs), out_shape=...]
where the time goes in v3:
time: 26.8 us; the launch traced here: 26.5 us
  Pallas kernels  23.4 us (87%)
  local copies, waits for them, and re-layouts  2.47 us (9%)
  between operations  0.65 us (2%)
    pallas_call x1, Pallas kernels, shards(): pl.pallas_call(functools.partial(kernel, owners, subs, pairs), out_shape=...  23.4 us
    unnamed x4, local copies, waits for them, and re-layouts  2.47 us

profile of v3, /device:TPU:1, one launch (start us, length us, event | category | flops | bytes accessed | tf_op | source)
XLA Modules:
  0.0 26.5 jit_solution(642795654239953899)
XLA Ops:
  0.6 23.4 %shard_map.77 = (f32[2,128,256]{2,1,0:T(8,128)}, f32[3,128,256]{2,1,0:T(8,128)}) custom-call(f32[5,32,1024]{2,1,0:T(8,128)} %dyn_ref.1, f32[5,32,1024]{2,1,0:T(8,128)} %area_ref.1, f32[5,32,1024]{2,1,0:T(8,128)} %vol_ref.1, s32[128]{0:T(128)} %block_ref.1, f32[2,128,256]{2,1,0:T(8,128)} %wind_ref.1, s32[128,256]{1,0:T(8,128)} %mask_ref.1), custom_call_target="tpu_custom_call" | custom-call | tf_op jit(solution)/shard_map/pallas_call | solution.py:438
  24.1 0.0 copy-start
  24.1 1.7 %copy.10 = f32[2,128,256]{2,1,0:T(8,128)} copy(f32[2,128,256]{2,1,0:T(8,128)} %get-tuple-element.4) | data formatting | bytes 524288
  25.8 0.0 copy-done
  25.8 0.7 %copy.11 = f32[3,128,256]{2,1,0:T(8,128)} copy(f32[3,128,256]{2,1,0:T(8,128)S(1)} %copy-done) | data formatting | bytes 786432
Async XLA Ops:
  24.1 1.7 %copy-start = (f32[3,128,256]{2,1,0:T(8,128)S(1)}, f32[3,128,256]{2,1,0:T(8,128)}, u32[]{:S(2)}) copy-start(f32[3,128,256]{2,1,0:T(8,128)} %get-tuple-element.5) | copy-start | bytes 1179652

commit v4 on v3

--- a/solution.py
+++ b/solution.py
@@ -28,7 +28,7 @@
 TALL = LOW + HALO + 8
 SPAN = ROWS + 2 * HALO
 STEP = 32
-PIECE = 16
+PIECE = 8
 UNROLL = True
 LIMIT = 56
 FIELDS = 7
@@ -39,7 +39,7 @@
     owners, subs, pairs,
     dyn_ref, area_ref, vol_ref, block_ref, wind_ref, mask_ref,
     vel_out, stress_out,
-    vel_ref, stress_ref, fixed_ref, final, own, area, vol, send, came, grid, mask, edge, side, source,
+    vel_ref, stress_ref, fixed_ref, own, area, vol, send, came, grid, mask, edge, side, source,
     in_sem, out_sem, mig_send, mig_recv, halo_send, halo_recv,
 ):
     me = lax.axis_index("curve")
@@ -205,7 +205,8 @@
     odd = lax.rem(lax.div(lane, BS), 2) == 1
     arrivals = came.reshape(owners * MOST, FIELDS, CHUNKS, LANES)
 
-    def settle(r, carry):
+    def settle(i, carry):
+        r = lax.rem(i * (RB - 1), RB)
         for h in range(TILES):
             slots = []
             for m in range(PER):
@@ -230,11 +231,12 @@
                     grid[f, h, pl.ds(CORE + r * BS + y, CHUNKS, stride=PER), :] = value
         return carry
 
-    lax.fori_loop(0, RB, settle, 0)
+    lax.fori_loop(0, 2, settle, 0)
 
     late = [(exists(-1, 0), row_copy(-1, 0, FIELDS, 2)), (exists(1, 0), row_copy(1, 0, FIELDS, 3))]
     late_back = [(exists(1, 0), late[0][1]), (exists(-1, 0), late[1][1])]
     each(late, lambda copy: copy.start())
+    lax.fori_loop(2, RB, settle, 0)
 
     def strips(i, carry):
         start = pl.multiple_of(i * STEP, 8)
@@ -278,16 +280,16 @@
         turning = 0.5 * mass
         scale = active / (drag * drag + turning * turning)
         keep = active * (1.0 / 1.5)
-        vel_ref[0, t, rows, :] = u
-        vel_ref[1, t, rows, :] = v
-        stress_ref[0, t, rows, :] = 0.25 * s1
-        stress_ref[1, t, rows, :] = 0.25 * s2
-        stress_ref[2, t, rows, :] = 0.5 * s12
+        vel_ref[0, t, rows, :] = 0.5 * u
+        vel_ref[1, t, rows, :] = 0.5 * v
+        stress_ref[0, t, rows, :] = 0.125 * s1
+        stress_ref[1, t, rows, :] = 0.125 * s2
+        stress_ref[2, t, rows, :] = 0.25 * s12
         fixed_ref[0, t, rows, :] = keep
-        fixed_ref[1, t, rows, :] = 0.125 * keep * strength
+        fixed_ref[1, t, rows, :] = 0.0625 * keep * strength
         fixed_ref[2, t, rows, :] = mass
-        fixed_ref[3, t, rows, :] = wind_x
-        fixed_ref[4, t, rows, :] = wind_y
+        fixed_ref[3, t, rows, :] = 0.5 * wind_x
+        fixed_ref[4, t, rows, :] = 0.5 * wind_y
         fixed_ref[5, t, rows, :] = scale * drag
         fixed_ref[6, t, rows, :] = scale * turning
 
@@ -321,7 +323,7 @@
 
     lax.fori_loop(0, SPAN // STEP, spread, 0)
 
-    cycles(vel_out, stress_out, vel_ref, stress_ref, fixed_ref, final, out_sem)
+    cycles(vel_out, stress_out, vel_ref, stress_ref, fixed_ref, out_sem)
 
     def sent(k, carry):
         migrate(k).wait_send()
@@ -331,7 +333,7 @@
     each(early + late + columns, lambda copy: copy.wait_send())
 
 
-def cycles(vel_out, stress_out, vel, stress, fixed, final, out_sem):
+def cycles(vel_out, stress_out, vel, stress, fixed, out_sem):
     tiles = range(TILES + 1)
     place = lax.broadcasted_iota(jnp.int32, (PIECE, LANES), 1)
     is_first, is_last = place == 0, place == LANES - 1
@@ -358,7 +360,7 @@
                 divergence = u_x[t] + v_y
                 tension = u_x[t] - v_y
                 shearing = u_y + v_x[t]
-                inverse = lax.rsqrt(divergence * divergence + 0.25 * (tension * tension + shearing * shearing) + 1.0)
+                inverse = lax.rsqrt(divergence * divergence + 0.25 * (tension * tension + shearing * shearing) + 0.25)
                 keep = fixed[0, t, rows, :]
                 force = fixed[1, t, rows, :]
                 scaled = force * inverse
@@ -403,7 +405,7 @@
     stores = []
     for t in range(TILES):
         stores.append(pltpu.make_async_copy(
-            final.at[:, t], stress_out.at[:, :, pl.ds(t * LANES, LANES)], out_sem.at[t]))
+            stress.at[:, t, pl.ds(CORE, ROWS), :], stress_out.at[:, :, pl.ds(t * LANES, LANES)], out_sem.at[t]))
     for t in range(TILES):
         stores.append(pltpu.make_async_copy(
             vel.at[:, t, pl.ds(CORE, ROWS), :], vel_out.at[:, :, pl.ds(t * LANES, LANES)],
@@ -421,12 +423,8 @@
 
     lax.fori_loop(0, 2, early, 0)
     lax.fori_loop(2, SUB, subcycle, 0)
-    for store in stores[TILES:]:
+    for store in stores:
         store.start()
-    for t in range(TILES):
-        for f, factor in enumerate((4.0, 4.0, 2.0)):
-            final[f, t] = factor * stress[f, t, pl.ds(CORE, ROWS), :]
-        stores[t].start()
     for store in stores:
         store.wait()
 
@@ -435,7 +433,7 @@
     owners, subs, pairs = (lax.axis_size(name) for name in ("curve", "sub", "pair"))
     anywhere = pl.BlockSpec(memory_space=pl.ANY)
     real = jnp.float32
-    return pl.pallas_call(
+    velocity, stress = pl.pallas_call(
         functools.partial(kernel, owners, subs, pairs),
         out_shape=(
             jax.ShapeDtypeStruct((2, ROWS, CB * BS), real),
@@ -447,7 +445,6 @@
             pltpu.VMEM((2, TILES + 1, TALL, LANES), real),
             pltpu.VMEM((3, TILES + 1, TALL, LANES), real),
             pltpu.VMEM((7, TILES + 1, TALL, LANES), real),
-            pltpu.VMEM((3, TILES, ROWS, LANES), real),
             pltpu.VMEM((CHUNKS, FIELDS, SLOT, LANES), real),
             pltpu.VMEM((CHUNKS, NCAT, SLOT, LANES), real),
             pltpu.VMEM((CHUNKS, NCAT, SLOT, LANES), real),
@@ -469,6 +466,8 @@
             collective_id=0, has_side_effects=True, vmem_limit_bytes=LIMIT * 1024 * 1024
         ),
     )(old_dynamics, old_area, old_volume, old_block, wind_stress, ice_mask)
+    factors = jnp.array([8.0, 8.0, 4.0], real).reshape(3, 1, 1)
+    return 2.0 * velocity, factors * stress
 
 
 def solution(mesh):

time: 26.8 us -> 26.3 us (0.981)
  other arithmetic: 0 us -> 2.56 us
  local copies, waits for them, and re-layouts: 2.47 us -> 0.01 us
  Pallas kernels: 23.4 us -> 22.9 us
    mul x0 -> x2, other arithmetic: none -> 2.56 us  [shards(): return (2.0 * velocity, factors * stress)]
    unnamed x4, local copies, waits for them, and re-layouts: 2.47 us -> 0.01 us
    pallas_call x1, Pallas kernels: 23.4 us -> 22.9 us  [shards(): pl.pallas_call(functools.partial(kernel, owners, subs, pairs), out_shape=...]
where the time goes in v4:
time: 26.3 us; the launch traced here: 26.1 us
  Pallas kernels  22.9 us (87%)
  other arithmetic  2.56 us (10%)
  between operations  0.66 us (3%)
    pallas_call x1, Pallas kernels, shards(): pl.pallas_call(functools.partial(kernel, owners, subs, pairs), out_shape=...  22.9 us
    mul x2, other arithmetic, shards(): return (2.0 * velocity, factors * stress)  2.56 us

profile of v4, /device:TPU:1, one launch (start us, length us, event | category | flops | bytes accessed | tf_op | source)
XLA Modules:
  0.0 26.1 jit_solution(11641378718492119573)
XLA Ops:
  0.6 22.9 %shard_map.86 = (f32[2,128,256]{2,1,0:T(8,128)}, f32[3,128,256]{2,1,0:T(8,128)}) custom-call(f32[5,32,1024]{2,1,0:T(8,128)} %dyn_ref.1, f32[5,32,1024]{2,1,0:T(8,128)} %area_ref.1, f32[5,32,1024]{2,1,0:T(8,128)} %vol_ref.1, s32[128]{0:T(128)} %block_ref.1, f32[2,128,256]{2,1,0:T(8,128)} %wind_ref.1, s32[128,256]{1,0:T(8,128)} %mask_ref.1), custom_call_target="tpu_custom_call" | custom-call | tf_op jit(solution)/shard_map/pallas_call | solution.py:436
  23.5 0.0 copy-start
  23.5 0.0 copy-start.1
  23.6 1.7 %broadcast_multiply_fusion.1 = f32[2,128,256]{2,1,0:T(8,128)} fusion(f32[2,128,256]{2,1,0:T(8,128)} %get-tuple-element.4), kind=kLoop, calls=%fused_computation.1 | loop fusion | flops 65536 | bytes 524288 | tf_op jit(solution)/shard_map/mul | solution.py:470
  25.3 0.0 copy-done
  25.3 0.0 copy-done.1
  25.3 0.8 %broadcast_multiply_fusion = f32[3,128,256]{2,1,0:T(8,128)} fusion(f32[3,128,256]{2,1,0:T(8,128)S(1)} %copy-done, f32[3]{0:T(128)S(1)} %copy-done.1), kind=kLoop, calls=%fused_computation | loop fusion | flops 98304 | bytes 786444 | tf_op jit(solution)/shard_map/mul | solution.py:470
Async XLA Ops:
  23.5 1.7 %copy-start = (f32[3,128,256]{2,1,0:T(8,128)S(1)}, f32[3,128,256]{2,1,0:T(8,128)}, u32[]{:S(2)}) copy-start(f32[3,128,256]{2,1,0:T(8,128)} %get-tuple-element.5) | copy-start | bytes 1179652
  23.5 1.7 %copy-start.1 = (f32[3]{0:T(128)S(1)}, f32[3]{0:T(128)}, u32[]{:S(2)}) copy-start(f32[3]{0:T(128)} %constant.4.clone) | copy-start | bytes 40

commit v5 on v4

--- a/solution.py
+++ b/solution.py
@@ -122,7 +122,7 @@
 
     lax.fori_loop(0, CHUNKS, derive, 0)
 
-    flat = own.reshape(CHUNKS * FIELDS * SLOT, LANES)
+    flat = own.reshape((CHUNKS + 1) * FIELDS * SLOT, LANES)
 
     def block_rows(field, slot):
         return flat[pl.ds(field * SLOT + slot, CHUNKS, stride=FIELDS * SLOT), :]
@@ -445,7 +445,7 @@
             pltpu.VMEM((2, TILES + 1, TALL, LANES), real),
             pltpu.VMEM((3, TILES + 1, TALL, LANES), real),
             pltpu.VMEM((7, TILES + 1, TALL, LANES), real),
-            pltpu.VMEM((CHUNKS, FIELDS, SLOT, LANES), real),
+            pltpu.VMEM((CHUNKS + 1, FIELDS, SLOT, LANES), real),
             pltpu.VMEM((CHUNKS, NCAT, SLOT, LANES), real),
             pltpu.VMEM((CHUNKS, NCAT, SLOT, LANES), real),
             pltpu.VMEM((owners, MOST, FIELDS, CHUNKS, LANES), real),

time: 26.3 us -> 26.3 us (level)
  no operation moved by 1% of the time
where the time goes in v5:
time: 26.3 us; the launch traced here: 26.1 us
  Pallas kernels  22.9 us (87%)
  other arithmetic  2.56 us (10%)
  between operations  0.66 us (3%)
    pallas_call x1, Pallas kernels, shards(): pl.pallas_call(functools.partial(kernel, owners, subs, pairs), out_shape=...  22.9 us
    mul x2, other arithmetic, shards(): return (2.0 * velocity, factors * stress)  2.56 us

profile of v5, /device:TPU:1, one launch (start us, length us, event | category | flops | bytes accessed | tf_op | source)
XLA Modules:
  0.0 26.1 jit_solution(18369013384379058890)
XLA Ops:
  0.6 22.9 %shard_map.86 = (f32[2,128,256]{2,1,0:T(8,128)}, f32[3,128,256]{2,1,0:T(8,128)}) custom-call(f32[5,32,1024]{2,1,0:T(8,128)} %dyn_ref.1, f32[5,32,1024]{2,1,0:T(8,128)} %area_ref.1, f32[5,32,1024]{2,1,0:T(8,128)} %vol_ref.1, s32[128]{0:T(128)} %block_ref.1, f32[2,128,256]{2,1,0:T(8,128)} %wind_ref.1, s32[128,256]{1,0:T(8,128)} %mask_ref.1), custom_call_target="tpu_custom_call" | custom-call | tf_op jit(solution)/shard_map/pallas_call | solution.py:436
  23.5 0.0 copy-start
  23.5 0.0 copy-start.1
  23.6 1.7 %broadcast_multiply_fusion.1 = f32[2,128,256]{2,1,0:T(8,128)} fusion(f32[2,128,256]{2,1,0:T(8,128)} %get-tuple-element.4), kind=kLoop, calls=%fused_computation.1 | loop fusion | flops 65536 | bytes 524288 | tf_op jit(solution)/shard_map/mul | solution.py:470
  25.3 0.0 copy-done
  25.3 0.0 copy-done.1
  25.3 0.8 %broadcast_multiply_fusion = f32[3,128,256]{2,1,0:T(8,128)} fusion(f32[3,128,256]{2,1,0:T(8,128)S(1)} %copy-done, f32[3]{0:T(128)S(1)} %copy-done.1), kind=kLoop, calls=%fused_computation | loop fusion | flops 98304 | bytes 786444 | tf_op jit(solution)/shard_map/mul | solution.py:470
Async XLA Ops:
  23.5 1.7 %copy-start = (f32[3,128,256]{2,1,0:T(8,128)S(1)}, f32[3,128,256]{2,1,0:T(8,128)}, u32[]{:S(2)}) copy-start(f32[3,128,256]{2,1,0:T(8,128)} %get-tuple-element.5) | copy-start | bytes 1179652
  23.5 1.7 %copy-start.1 = (f32[3]{0:T(128)S(1)}, f32[3]{0:T(128)}, u32[]{:S(2)}) copy-start(f32[3]{0:T(128)} %constant.4.clone) | copy-start | bytes 40
